TPU v7x, 32 devices: a whole 2x2x4 slice. The times are simulated.
32 devices in a mesh: dp: 16 (over z, y, x), tensor: 2 (over core).
Axes of the slice: x: 2, y: 2, z: 4, core: 2. Of those that a mesh axis runs over, the one named last changes fastest.
Arguments:
- tokens: bfloat16 [16384, 768], P(('dp', 'tensor')), may hold values from -6 to 6
- qkv_weight: bfloat16 [768, 3, 768], P(None, None, 'tensor'), may hold values from -0.21875 to 0.21875
- qv_bias: float32 [2, 768], P(None, 'tensor'), may hold values from -3 to 3
- rel_table: float32 [256, 12], P(None, 'tensor'), may hold values from -4 to 4
- out_weight: bfloat16 [768, 768], P('tensor'), may hold values from -1.25 to 1.25
- out_bias: float32 [768], replicated, may hold values from -3 to 3
- norm1_gain: float32 [768], replicated, may hold values from 0.5 to 1.5
- norm1_bias: float32 [768], replicated, may hold values from -3 to 3
- up_weight: bfloat16 [768, 3072], P(None, 'tensor'), may hold values from -0.21875 to 0.21875
- up_bias: float32 [3072], P('tensor'), may hold values from -3 to 3
- down_weight: bfloat16 [3072, 768], P('tensor'), may hold values from -0.109375 to 0.109375
- down_bias: float32 [768], replicated, may hold values from -3 to 3
- norm2_gain: float32 [768], replicated, may hold values from 0.5 to 1.5
- norm2_bias: float32 [768], replicated, may hold values from -3 to 3
- rel_bucket: int32 [512, 512], replicated, may hold values from 0 to 127
- query_len: int32 [32], P('dp'), may hold values from 1 to 128
- key_mask: int32 [32, 512], P('dp'), may hold values from 0 to 1, as said below
- upstream: bfloat16 [16384, 768], P(('dp', 'tensor')), may hold values from -6 to 6
Outputs:
- out: bfloat16 [16384, 768], P(('dp', 'tensor'))
- grad_tokens: float32 [16384, 768], P(('dp', 'tensor'))
- grad_qkv_weight: float32 [768, 3, 768], P(None, None, 'tensor')
- grad_qv_bias: float32 [2, 768], P(None, 'tensor')
- grad_rel_table: float32 [256, 12], P(None, 'tensor')
- grad_out_weight: float32 [768, 768], P('tensor')
- grad_out_bias: float32 [768], replicated
- grad_norm1_gain: float32 [768], replicated
- grad_norm1_bias: float32 [768], replicated
- grad_up_weight: float32 [768, 3072], P(None, 'tensor')
- grad_up_bias: float32 [3072], P('tensor')
- grad_down_weight: float32 [3072, 768], P('tensor')
- grad_down_bias: float32 [768], replicated
- grad_norm2_gain: float32 [768], replicated
- grad_norm2_bias: float32 [768], replicated
Inputs may be any that keep to these rules, and one draw needn't show every extreme that they name: Each row of key_mask is 1 on its first positions and 0 after them, with 256 or more ones; in every draw some pair has no padding.
All inputs are finite; a program needn't handle non-finite values.
Results may differ from a plain program's by a relative error of at most 0.017.
The roundings to bfloat16 on the way count: a program that leaves them out, or rounds other values in their place, can miss the bound.
Values may be sent and summed in bfloat16 or wider, within the bound.
A program may use at most 192 MiB of HBM per device.

v0:
```python
from functools import partial
import math

import jax
import jax.numpy as jnp
from jax import lax
from jax.sharding import PartitionSpec as P

EPSILON = 1e-05
FAR_BELOW = -1000000000.0


def exact_gelu(values):
    return jax.nn.gelu(values, approximate=False)


def layer_norm(values, gain, shift):
    center = values - jnp.mean(values, axis=-1, keepdims=True)
    inverse = lax.rsqrt(jnp.mean(center * center, axis=-1, keepdims=True) + EPSILON)
    normed = center * inverse
    return (normed * gain + shift, normed, inverse)


def norm_back(grad, normed, inverse, gain):
    scaled = grad * gain
    grad_in = inverse * (
        scaled
        - jnp.mean(scaled, axis=-1, keepdims=True)
        - normed * jnp.mean(scaled * normed, axis=-1, keepdims=True)
    )
    return (grad_in, jnp.sum(grad * normed, axis=0), jnp.sum(grad, axis=0))


def contract_rows(left, right):
    return lax.dot_general(
        left, right, (((0,), (0,)), ((), ())), preferred_element_type=jnp.float32
    )


def contract_cols(left, right):
    return lax.dot_general(
        left, right, (((1,), (1,)), ((), ())), preferred_element_type=jnp.float32
    )


def row_block(seq_len):
    return math.gcd(seq_len, 64)


def position_terms(table, rel_bucket):
    halfway = table.shape[0] // 2
    heads = table.shape[1]
    seq_len = rel_bucket.shape[0]
    block = row_block(seq_len)
    halves = table.reshape(2, halfway, heads)
    labels = jnp.arange(halfway, dtype=jnp.int32)

    def position_bucket_rows(indices):
        onehot = (indices[:, :, None] == labels[None, None, :]).astype(jnp.float32)
        return jnp.einsum("ijb,cbh->chij", onehot, halves, precision=lax.Precision.HIGHEST)

    blocks_out = lax.map(position_bucket_rows, rel_bucket.reshape(seq_len // block, block, seq_len))
    return jnp.transpose(blocks_out, (1, 2, 0, 3, 4)).reshape(2, heads, seq_len, seq_len)


def fold_table(grad_terms, rel_bucket, buckets):
    heads = grad_terms.shape[1]
    seq_len = rel_bucket.shape[0]
    halfway = buckets // 2
    block = row_block(seq_len)
    count = seq_len // block
    labels = jnp.arange(halfway, dtype=jnp.int32)
    grouped = jnp.transpose(grad_terms.reshape(2, heads, count, block, seq_len), (2, 0, 1, 3, 4))

    def fold_bucket_rows(items):
        indices, grads = items
        onehot = (indices[:, :, None] == labels[None, None, :]).astype(jnp.float32)
        return jnp.einsum("ijb,chij->cbh", onehot, grads, precision=lax.Precision.HIGHEST)

    partial_sums = lax.map(fold_bucket_rows, (rel_bucket.reshape(count, block, seq_len), grouped))
    return jnp.sum(partial_sums, axis=0).reshape(buckets, heads)


def pair_scores(query, keys, terms, length, valid):
    position = jnp.arange(terms.shape[-1], dtype=jnp.int32)
    segment = position < length
    crossing = segment[:, None] != segment[None, :]
    bias = jnp.where(crossing[None], terms[1], terms[0])
    scores = jnp.einsum("ihd,jhd->hij", query, keys, preferred_element_type=jnp.float32)
    return (jnp.where(valid[None, None, :] > 0, scores + bias, FAR_BELOW), crossing)


def pair_forward(terms, items):
    query, keys, values, length, valid = items
    scores, crossing = pair_scores(query, keys, terms, length, valid)
    highest = jnp.max(scores, axis=-1, keepdims=True)
    expo = jnp.exp(scores - highest)
    total = jnp.sum(expo, axis=-1, keepdims=True)
    chances = expo / total
    attended = jnp.einsum(
        "hij,jhd->ihd", chances.astype(jnp.bfloat16), values, preferred_element_type=jnp.float32
    )
    return (attended, highest + jnp.log(total))


def pair_backward(terms, gathered_terms, items):
    query, keys, values, grad_heads, log_total, length, valid = items
    scores, crossing = pair_scores(query, keys, terms, length, valid)
    chances = jnp.exp(scores - log_total)
    grad_chances = jnp.einsum(
        "ihd,jhd->hij", grad_heads, values, preferred_element_type=jnp.float32
    )
    grad_scores = chances * (grad_chances - jnp.sum(chances * grad_chances, axis=-1, keepdims=True))
    zeros = jnp.zeros_like(grad_scores)
    split_grads = jnp.stack(
        [
            jnp.where(crossing[None], zeros, grad_scores),
            jnp.where(crossing[None], grad_scores, zeros),
        ]
    )
    low_scores = grad_scores.astype(jnp.bfloat16)
    grad_query = jnp.einsum(
        "hij,jhd->ihd", low_scores, keys, preferred_element_type=jnp.float32
    ).astype(jnp.bfloat16)
    grad_keys = jnp.einsum(
        "hij,ihd->jhd", low_scores, query, preferred_element_type=jnp.float32
    ).astype(jnp.bfloat16)
    grad_values = jnp.einsum(
        "hij,ihd->jhd", chances.astype(jnp.bfloat16), grad_heads, preferred_element_type=jnp.float32
    ).astype(jnp.bfloat16)
    return (gathered_terms + split_grads, (grad_query, grad_keys, grad_values))


def on_device(
    tokens,
    qkv_weight,
    qv_bias,
    rel_table,
    out_weight,
    out_bias,
    norm1_gain,
    norm1_bias,
    up_weight,
    up_bias,
    down_weight,
    down_bias,
    norm2_gain,
    norm2_bias,
    rel_bucket,
    query_len,
    key_mask,
    upstream,
):
    width = tokens.shape[1]
    heads = rel_table.shape[1]
    inner = qkv_weight.shape[2]
    head_size = inner // heads
    pairs = key_mask.shape[0]
    seq_len = key_mask.shape[1]
    mixed_weight = qkv_weight.reshape(width, 3 * inner)
    shape = (pairs, seq_len, heads, head_size)
    terms = position_terms(rel_table, rel_bucket)

    def forward(params):
        (
            layer_in,
            weight_mixed,
            shift_qv,
            weight_out,
            bias_out,
            gain_one,
            shift_one,
            weight_up,
            bias_up,
            weight_down,
            bias_down,
            gain_two,
            shift_two,
        ) = params
        gathered = lax.all_gather(layer_in, "tensor", axis=0, tiled=True)
        mixed = jnp.dot(gathered, weight_mixed, preferred_element_type=jnp.float32)
        query = ((mixed[:, :inner] + shift_qv[0]) * 0.125).astype(jnp.bfloat16)
        keys = mixed[:, inner : 2 * inner].astype(jnp.bfloat16)
        values = (mixed[:, 2 * inner :] + shift_qv[1]).astype(jnp.bfloat16)
        attended, log_total = lax.map(
            partial(pair_forward, terms),
            (query.reshape(shape), keys.reshape(shape), values.reshape(shape), query_len, key_mask),
        )
        heads_out = attended.reshape(pairs * seq_len, inner).astype(jnp.bfloat16)
        attention = lax.psum_scatter(
            jnp.dot(heads_out, weight_out, preferred_element_type=jnp.float32),
            "tensor",
            scatter_dimension=0,
            tiled=True,
        )
        first, normed_one, inverse_one = layer_norm(
            attention + bias_out + layer_in.astype(jnp.float32), gain_one, shift_one
        )
        hidden_in = lax.all_gather(first.astype(jnp.bfloat16), "tensor", axis=0, tiled=True)
        hidden = jnp.dot(hidden_in, weight_up, preferred_element_type=jnp.float32) + bias_up
        activated = exact_gelu(hidden).astype(jnp.bfloat16)
        branch = lax.psum_scatter(
            jnp.dot(activated, weight_down, preferred_element_type=jnp.float32).astype(
                jnp.bfloat16
            ),
            "tensor",
            scatter_dimension=0,
            tiled=True,
        ).astype(jnp.float32)
        result, normed_two, inverse_two = layer_norm(
            branch + bias_down + first, gain_two, shift_two
        )
        return (
            result,
            (
                gathered,
                query,
                keys,
                values,
                log_total,
                heads_out,
                normed_one,
                inverse_one,
                hidden_in,
                hidden,
                activated,
                normed_two,
                inverse_two,
            ),
        )

    params = (
        tokens,
        mixed_weight,
        qv_bias,
        out_weight,
        out_bias,
        norm1_gain,
        norm1_bias,
        up_weight,
        up_bias,
        down_weight,
        down_bias,
        norm2_gain,
        norm2_bias,
    )
    result, first_saved = forward(params)
    saved = forward(lax.optimization_barrier(params))[1]
    (
        gathered,
        query,
        keys,
        values,
        log_total,
        heads_out,
        normed_one,
        inverse_one,
        hidden_in,
        hidden,
        activated,
        normed_two,
        inverse_two,
    ) = saved
    grad_second, grad_gain_two, grad_shift_two = norm_back(
        upstream.astype(jnp.float32), normed_two, inverse_two, norm2_gain
    )
    grad_down_bias = jnp.sum(grad_second, axis=0)
    branch_rows = lax.all_gather(grad_second.astype(jnp.bfloat16), "tensor", axis=0, tiled=True)
    grad_down = contract_rows(activated, branch_rows)
    grad_activated = contract_cols(branch_rows, down_weight)
    gelu_back = jax.vjp(exact_gelu, hidden)[1]
    grad_hidden = gelu_back(grad_activated)[0].astype(jnp.bfloat16)
    grad_up = contract_rows(hidden_in, grad_hidden)
    grad_up_bias = jnp.sum(grad_hidden, axis=0, dtype=jnp.float32)
    grad_first = grad_second + lax.psum_scatter(
        contract_cols(grad_hidden, up_weight).astype(jnp.bfloat16),
        "tensor",
        scatter_dimension=0,
        tiled=True,
    ).astype(jnp.float32)
    grad_mid, grad_gain_one, grad_shift_one = norm_back(
        grad_first, normed_one, inverse_one, norm1_gain
    )
    grad_out_bias = jnp.sum(grad_mid, axis=0)
    mid_rows = lax.all_gather(grad_mid.astype(jnp.bfloat16), "tensor", axis=0, tiled=True)
    grad_out = contract_rows(heads_out, mid_rows)
    grad_heads = contract_cols(mid_rows, out_weight).astype(jnp.bfloat16)
    start_terms = jnp.zeros((2, heads, seq_len, seq_len), jnp.float32)
    term_grads, pieces = lax.scan(
        partial(pair_backward, terms),
        start_terms,
        (
            query.reshape(shape),
            keys.reshape(shape),
            values.reshape(shape),
            grad_heads.reshape(shape),
            log_total,
            query_len,
            key_mask,
        ),
    )
    grad_query, grad_keys, grad_values = pieces
    grad_table = fold_table(term_grads, rel_bucket, rel_table.shape[0])
    grad_query = grad_query.reshape(pairs * seq_len, inner) * jnp.bfloat16(0.125)
    grad_values = grad_values.reshape(pairs * seq_len, inner)
    grad_mixed = jnp.concatenate(
        [grad_query, grad_keys.reshape(pairs * seq_len, inner), grad_values], axis=1
    )
    grad_weight_mixed = contract_rows(gathered, grad_mixed)
    grad_qv = jnp.stack(
        [
            jnp.sum(grad_query, axis=0, dtype=jnp.float32),
            jnp.sum(grad_values, axis=0, dtype=jnp.float32),
        ]
    )
    grad_tokens = grad_mid + lax.psum_scatter(
        contract_cols(grad_mixed, mixed_weight).astype(jnp.bfloat16),
        "tensor",
        scatter_dimension=0,
        tiled=True,
    ).astype(jnp.float32)
    weight_sums = lax.psum(
        (grad_weight_mixed, grad_qv, grad_table, grad_out, grad_up, grad_up_bias, grad_down), "dp"
    )
    vector_sums = lax.psum(
        (
            grad_out_bias,
            grad_gain_one,
            grad_shift_one,
            grad_down_bias,
            grad_gain_two,
            grad_shift_two,
        ),
        ("dp", "tensor"),
    )
    return (
        result.astype(jnp.bfloat16),
        grad_tokens,
        weight_sums[0].reshape(width, 3, inner),
        weight_sums[1],
        weight_sums[2],
        weight_sums[3],
        vector_sums[0],
        vector_sums[1],
        vector_sums[2],
        weight_sums[4],
        weight_sums[5],
        weight_sums[6],
        vector_sums[3],
        vector_sums[4],
        vector_sums[5],
    )


def solution(mesh):
    in_specs = (
        P(("dp", "tensor"), None),
        P(None, None, "tensor"),
        P(None, "tensor"),
        P(None, "tensor"),
        P("tensor", None),
        P(),
        P(),
        P(),
        P(None, "tensor"),
        P("tensor"),
        P("tensor", None),
        P(),
        P(),
        P(),
        P(),
        P("dp"),
        P("dp", None),
        P(("dp", "tensor"), None),
    )
    out_specs = (
        P(("dp", "tensor"), None),
        P(("dp", "tensor"), None),
        P(None, None, "tensor"),
        P(None, "tensor"),
        P(None, "tensor"),
        P("tensor", None),
        P(),
        P(),
        P(),
        P(None, "tensor"),
        P("tensor"),
        P("tensor", None),
        P(),
        P(),
        P(),
    )
    return jax.shard_map(
        on_device, mesh=mesh, in_specs=in_specs, out_specs=out_specs, check_vma=False
    )
```

profile of v0, /device:TPU:0, one launch (start us, length us, event | category | flops | bytes accessed | tf_op | source)
XLA Modules:
  0.0 970.4 jit_solution(14493449852114936312)
XLA Ops:
  11.3 107.7 %while.63 = (s32[]{:T(128)}, f32[8,2,6,64,512]{4,2,1,3,0:T(8,128)}, s32[8,64,512]{2,1,0:T(8,128)}, f32[2,128,6]{1,2,0:T(8,128)S(1)}, s32[]{:T(128)}) while((s32[]{:T(128)}, f32[8,2,6,64,512]{4,2,1,3,0:T(8,128)}, s32[8,64,512]{2,1,0:T(8,128)}, f32[2,128,6]{1,2,0:T(8,128)S(1)}, s32[]{:T(128)}) %tuple.186), condition=%wide.region_1.2_spmd.clone, body=%wide.region_0.1_spmd.clone.sunk | while | flops 608174080 | bytes 2496589 | solution.py:62
  12.3 12.5 %bitcast_dynamic-update-slice_fusion.5 = f32[8,2,6,64,512]{4,2,1,3,0:T(8,128)} fusion(f32[8,2,6,64,512]{4,2,1,3,0:T(8,128)} %get-tuple-element.833, s32[]{:T(128)S(6)} %copy.158, s32[64,512]{1,0:T(8,128)S(1)} %dynamic-slice_bitcast_fusion.6, f32[2,128,6]{1,2,0:T(8,128)S(1)} %get-tuple-element.840), kind=kOutput, calls=%fused_computation.6.clone.1 | convolution fusion | flops 608174080 | bytes 2234372 | tf_op jit(solution)/shard_map/while/body/eval_jaxpr/ijb,cbh->chij/dot_general | solution.py:60
  25.7 12.5 %bitcast_dynamic-update-slice_fusion.5 = f32[8,2,6,64,512]{4,2,1,3,0:T(8,128)} fusion(f32[8,2,6,64,512]{4,2,1,3,0:T(8,128)} %get-tuple-element.833, s32[]{:T(128)S(6)} %copy.158, s32[64,512]{1,0:T(8,128)S(1)} %dynamic-slice_bitcast_fusion.6, f32[2,128,6]{1,2,0:T(8,128)S(1)} %get-tuple-element.840), kind=kOutput, calls=%fused_computation.6.clone.1 | convolution fusion | flops 608174080 | bytes 2234372 | tf_op jit(solution)/shard_map/while/body/eval_jaxpr/ijb,cbh->chij/dot_general | solution.py:60
  39.2 12.5 %bitcast_dynamic-update-slice_fusion.5 = f32[8,2,6,64,512]{4,2,1,3,0:T(8,128)} fusion(f32[8,2,6,64,512]{4,2,1,3,0:T(8,128)} %get-tuple-element.833, s32[]{:T(128)S(6)} %copy.158, s32[64,512]{1,0:T(8,128)S(1)} %dynamic-slice_bitcast_fusion.6, f32[2,128,6]{1,2,0:T(8,128)S(1)} %get-tuple-element.840), kind=kOutput, calls=%fused_computation.6.clone.1 | convolution fusion | flops 608174080 | bytes 2234372 | tf_op jit(solution)/shard_map/while/body/eval_jaxpr/ijb,cbh->chij/dot_general | solution.py:60
  52.6 12.6 %bitcast_dynamic-update-slice_fusion.5 = f32[8,2,6,64,512]{4,2,1,3,0:T(8,128)} fusion(f32[8,2,6,64,512]{4,2,1,3,0:T(8,128)} %get-tuple-element.833, s32[]{:T(128)S(6)} %copy.158, s32[64,512]{1,0:T(8,128)S(1)} %dynamic-slice_bitcast_fusion.6, f32[2,128,6]{1,2,0:T(8,128)S(1)} %get-tuple-element.840), kind=kOutput, calls=%fused_computation.6.clone.1 | convolution fusion | flops 608174080 | bytes 2234372 | tf_op jit(solution)/shard_map/while/body/eval_jaxpr/ijb,cbh->chij/dot_general | solution.py:60
  66.1 12.5 %bitcast_dynamic-update-slice_fusion.5 = f32[8,2,6,64,512]{4,2,1,3,0:T(8,128)} fusion(f32[8,2,6,64,512]{4,2,1,3,0:T(8,128)} %get-tuple-element.833, s32[]{:T(128)S(6)} %copy.158, s32[64,512]{1,0:T(8,128)S(1)} %dynamic-slice_bitcast_fusion.6, f32[2,128,6]{1,2,0:T(8,128)S(1)} %get-tuple-element.840), kind=kOutput, calls=%fused_computation.6.clone.1 | convolution fusion | flops 608174080 | bytes 2234372 | tf_op jit(solution)/shard_map/while/body/eval_jaxpr/ijb,cbh->chij/dot_general | solution.py:60
  79.6 12.5 %bitcast_dynamic-update-slice_fusion.5 = f32[8,2,6,64,512]{4,2,1,3,0:T(8,128)} fusion(f32[8,2,6,64,512]{4,2,1,3,0:T(8,128)} %get-tuple-element.833, s32[]{:T(128)S(6)} %copy.158, s32[64,512]{1,0:T(8,128)S(1)} %dynamic-slice_bitcast_fusion.6, f32[2,128,6]{1,2,0:T(8,128)S(1)} %get-tuple-element.840), kind=kOutput, calls=%fused_computation.6.clone.1 | convolution fusion | flops 608174080 | bytes 2234372 | tf_op jit(solution)/shard_map/while/body/eval_jaxpr/ijb,cbh->chij/dot_general | solution.py:60
  93.0 12.5 %bitcast_dynamic-update-slice_fusion.5 = f32[8,2,6,64,512]{4,2,1,3,0:T(8,128)} fusion(f32[8,2,6,64,512]{4,2,1,3,0:T(8,128)} %get-tuple-element.833, s32[]{:T(128)S(6)} %copy.158, s32[64,512]{1,0:T(8,128)S(1)} %dynamic-slice_bitcast_fusion.6, f32[2,128,6]{1,2,0:T(8,128)S(1)} %get-tuple-element.840), kind=kOutput, calls=%fused_computation.6.clone.1 | convolution fusion | flops 608174080 | bytes 2234372 | tf_op jit(solution)/shard_map/while/body/eval_jaxpr/ijb,cbh->chij/dot_general | solution.py:60
  106.5 12.6 %bitcast_dynamic-update-slice_fusion.5 = f32[8,2,6,64,512]{4,2,1,3,0:T(8,128)} fusion(f32[8,2,6,64,512]{4,2,1,3,0:T(8,128)} %get-tuple-element.833, s32[]{:T(128)S(6)} %copy.158, s32[64,512]{1,0:T(8,128)S(1)} %dynamic-slice_bitcast_fusion.6, f32[2,128,6]{1,2,0:T(8,128)S(1)} %get-tuple-element.840), kind=kOutput, calls=%fused_computation.6.clone.1 | convolution fusion | flops 608174080 | bytes 2234372 | tf_op jit(solution)/shard_map/while/body/eval_jaxpr/ijb,cbh->chij/dot_general | solution.py:60
  119.0 17.5 %copy.100 = f32[2,6,512,512]{2,3,1,0:T(8,128)} copy(f32[2,6,512,512]{3,1,0,2:T(8,128)} %bitcast.317) | data formatting | bytes 25165824 | tf_op jit(solution)/shard_map/while | solution.py:185
  163.5 33.1 %while.62 = (s32[]{:T(128)}, bf16[2,512,6,64]{1,3,2,0:T(8,128)(2,1)}, f32[2,6,512,1]{2,1,3,0:T(8,128)S(1)}, bf16[2,512,6,64]{1,3,2,0:T(8,128)(2,1)}, s32[2,512]{...) while((s32[]{:T(128)}, ...), condition=%wide.region_15.16_spmd, body=%wide.region_12.15_spmd.sunk | while | flops 417069056 | bytes 43509976 | solution.py:185
  165.0 5.8 fusion.259
  175.8 5.8 fusion.259
  203.8 13.7 %reduce-scatter.11.cloned.1.call-done = f32[512,768]{1,0:T(8,128)} async-done(((f32[1024,768]{1,0:T(8,128)}), f32[512,768]{1,0:T(8,128)}) %reduce-scatter.11.cloned.1.call-update) | async-done | bytes 1572880 | tf_op jit(solution)/shard_map/reduce_scatter | solution.py:190
  222.4 10.5 %all-gather.13.cloned.1.call-done = bf16[1024,768]{1,0:T(8,128)(2,1)} async-done(((bf16[512,768]{1,0:T(8,128)(2,1)}), bf16[1024,768]{1,0:T(8,128)(2,1)}) %all-gather.13.cloned.1.call-update) | async-done | bytes 1572880 | tf_op jit(solution)/shard_map/all_gather | solution.py:199
  232.9 18.3 %multiply_convert_fusion = (bf16[1024,1536]{1,0:T(8,128)(2,1)S(1)}, f32[1024,1536]{1,0:T(8,128)}, f32[1024,1536]{1,0:T(8,128)}) fusion(f32[1536]{0:T(1024)S(1)} %copy-done.57, bf16[1024,768]{1,0:T(8,128)(2,1)} %all-gather.13.cloned.1.call-done, bf16[768,1536]{1,0:T(8,128)(2,1)S(1)} %copy-done), kind=kOutput, calls=%fused_computation.118 | convolution fusion | flops 2519728128 | bytes 19666944 | tf_op jit(solution)/shard_map/dot_general | solution.py:200
  289.7 38.9 %while.61 = (s32[]{:T(128)}, bf16[2,512,6,64]{1,3,2,0:T(8,128)(2,1)}, bf16[2,512,6,64]{1,3,2,0:T(8,128)(2,1)}, s32[2,512]{1,0:T(2,128)S(1)}, bf16[2,512,6,64]{1,...) while((s32[]{:T(128)}, ...), condition=%wide.region_5.6_spmd, body=%wide.region_2.5_spmd.sunk | while | flops 415503360 | bytes 65435796 | solution.py:185
  291.6 6.9 fusion.255
  302.4 7.1 fusion.257
  310.9 6.8 fusion.255
  321.6 7.1 fusion.257
  334.6 10.8 %convert_reduce_fusion = (f32[1536]{0:T(1024)}, bf16[1024,1536]{1,0:T(8,128)(2,1)S(1)}) fusion(f32[1024,1536]{1,0:T(8,128)} %get-tuple-element.563, f32[1024,1536]{1,0:T(8,128)} %get-tuple-element.579, f32[1536]{0:T(1024)S(1)} %copy-done.57, bf16[1024,768]{1,0:T(8,128)(2,1)} %all-gather.15.cloned.1.call-done, bf16[1536,768]{1,0:T(8,128)(2,1)} %param.38), kind=kOutput, calls=%fused_computation.116 | convolution fusion | flops 2442656256 | bytes 19673088 | tf_op jit(solution)/shard_map/dot_general | solution.py:41
  354.6 6.7 reduce-scatter.15.cloned.1.call-done
  366.0 11.1 %all-gather.9.cloned.1.call-done = bf16[1024,768]{1,0:T(8,128)(2,1)} async-done(((bf16[512,768]{1,0:T(8,128)(2,1)}), bf16[1024,768]{1,0:T(8,128)(2,1)}) %all-gather.9.cloned.1.call-update) | async-done | bytes 1572880 | tf_op jit(solution)/shard_map/all_gather | solution.py:199
  377.1 20.3 %fusion.127 = bf16[1024,768]{1,0:T(8,128)(2,1)} fusion(bf16[1536,768]{1,0:T(8,128)(2,1)} %param.38, bf16[1024,768]{1,0:T(8,128)(2,1)} %all-gather.9.cloned.1.call-done, bf16[768,1536]{1,0:T(8,128)(2,1)S(1)} %copy-done, f32[1536]{0:T(1024)S(1)} %copy-done.57), kind=kOutput, calls=%fused_computation.154 | convolution fusion | flops 4936433664 | bytes 7870464 | tf_op jit(solution)/shard_map/dot_general | solution.py:203
  397.4 10.3 %reduce-scatter.9.cloned.1.call-done = bf16[512,768]{1,0:T(8,128)(2,1)} async-done(((bf16[1024,768]{1,0:T(8,128)(2,1)}), bf16[512,768]{1,0:T(8,128)(2,1)}) %reduce-scatter.9.cloned.1.call-update) | async-done | bytes 786448 | tf_op jit(solution)/shard_map/reduce_scatter | solution.py:202
  414.1 10.8 %all-gather.17.cloned.1.call-done = bf16[1024,768]{1,0:T(8,128)(2,1)} async-done(((bf16[512,768]{1,0:T(8,128)(2,1)}), bf16[1024,768]{1,0:T(8,128)(2,1)}) %all-gather.17.cloned.1.call-update) | async-done | bytes 1572880 | tf_op jit(solution)/shard_map/all_gather | solution.py:285
  432.4 88.1 %while.65 = (s32[]{:T(128)}, f32[2,6,512,512]{2,3,1,0:T(8,128)}, bf16[2,512,6,64]{1,3,2,0:T(8,128)(2,1)}, bf16[2,512,6,64]{1,3,2,0:T(8,128)(2,1)}, bf16[2,512,6,...) while((s32[]{:T(128)}, f32[2,6,512,512]{2,3,1,0:T(8,128)}, ...), condition=%wide.region_29.30_spmd.clone, body=%wide.region_27.29_spmd.clone.sunk | while | flops 1037367296 | bytes 237839824 | solution.py:289
  436.0 8.5 multiply_reduce_fusion.9
  448.1 11.3 %select_bitcast_fusion.4 = (f32[1,6,512,512]{2,3,1,0:T(8,128)}, f32[6,512,512]{1,2,0:T(8,128)}) fusion(pred[512,512]{0,1:T(8,128)(4,1)S(1)} %broadcast_compare_fusion.8, f32[6,512,512]{1,2,0:T(8,128)} %copy-done.4, f32[6,512,512]{1,2,0:T(8,128)} %copy-done.3, f32[6,512]{1,0:T(8,128)S(1)} %get-tuple-element.824), kind=kLoop, calls=%fused_computation.67.clone.1 | loop fusion | flops 4718592 | bytes 25440256 | tf_op jit(solution)/shard_map/while/body/eval_jaxpr/stack | solution.py:115
  467.5 6.1 maximum_add_fusion.2
  477.2 8.5 multiply_reduce_fusion.9
  489.4 11.3 %select_bitcast_fusion.4 = (f32[1,6,512,512]{2,3,1,0:T(8,128)}, f32[6,512,512]{1,2,0:T(8,128)}) fusion(pred[512,512]{0,1:T(8,128)(4,1)S(1)} %broadcast_compare_fusion.8, f32[6,512,512]{1,2,0:T(8,128)} %copy-done.4, f32[6,512,512]{1,2,0:T(8,128)} %copy-done.3, f32[6,512]{1,0:T(8,128)S(1)} %get-tuple-element.824), kind=kLoop, calls=%fused_computation.67.clone.1 | loop fusion | flops 4718592 | bytes 25440256 | tf_op jit(solution)/shard_map/while/body/eval_jaxpr/stack | solution.py:115
  508.7 11.4 %maximum_add_fusion.2 = f32[2,6,512,512]{2,3,1,0:T(8,128)} fusion(f32[1,6,512,512]{2,3,1,0:T(8,128)S(1)} %select_bitcast_fusion.5, f32[1,6,512,512]{2,3,1,0:T(8,128)S(1)} %bitcast.315, f32[2,6,512,512]{2,3,1,0:T(8,128)} %get-tuple-element.915, pred[]{:T(512)S(6)} %compare.3), kind=kLoop, calls=%fused_computation.60.clone.1 | loop fusion | flops 9437184 | bytes 37748736 | tf_op jit(solution)/shard_map/while/body/eval_jaxpr/add | solution.py:131
  531.0 7.4 fusion.187
  550.0 44.5 %all-reduce = (f32[768]{0:T(1024)}, f32[768]{0:T(1024)}, f32[768]{0:T(1024)}, f32[768]{0:T(1024)}, f32[768]{0:T(1024)}, /*index=5*/f32[768]{0:T(1024)}) all-reduce(f32[768]{0:T(1024)S(1)} %copy-done.48, f32[768]{0:T(1024)S(1)} %copy-done.45, f32[768]{0:T(1024)S(1)} %copy-done.46, ...), channel_id=1, replica_groups=mesh['dp'=16,'tensor'=2] {'dp','tensor'}, use_global_device_ids=true, to_apply=%region_41.42 | all-reduce | flops 4608 | bytes 36864 | tf_op jit(solution)/shard_map/psum | solution.py:325
  596.0 12.8 %copy.120 = f32[2,6,512,512]{3,2,1,0:T(8,128)} copy(f32[2,6,512,512]{2,3,1,0:T(8,128)} %get-tuple-element.258) | data formatting | bytes 25165824 | tf_op jit(solution)/shard_map/while | solution.py:289
  609.4 125.5 %while.64 = (s32[]{:T(128)}, f32[8,2,128,6]{2,3,1,0:T(8,128)S(1)}, f32[8,2,6,64,512]{4,3,0,2,1:T(8,128)}, s32[8,64,512]{2,1,0:T(8,128)}, s32[]{:T(128)}) while((s32[]{:T(128)}, f32[8,2,128,6]{2,3,1,0:T(8,128)S(1)}, f32[8,2,6,64,512]{4,3,0,2,1:T(8,128)}, s32[8,64,512]{2,1,0:T(8,128)}, s32[]{:T(128)}) %tuple.181), condition=%wide.region_36.37_spmd.clone, body=%wide.region_35.36_spmd.clone.sunk | while | flops 608174080 | bytes 5120081 | solution.py:80
  611.9 13.2 %fusion.265 = f32[8,2,128,6]{2,3,1,0:T(8,128)S(1)} fusion(f32[8,2,128,6]{2,3,1,0:T(8,128)S(1)} %get-tuple-element.950, s32[]{:T(128)S(6)} %copy.200, s32[64,512]{1,0:T(8,128)S(1)} %dynamic-slice_bitcast_fusion.7, f32[1,2,6,64,512]{4,3,0,2,1:T(8,128)S(1)} %constant_dynamic-slice_fusion.3), kind=kOutput, calls=%fused_computation.15.clone.1 | convolution fusion | flops 608174080 | bytes 1712132 | tf_op jit(solution)/shard_map/while/body/eval_jaxpr/ijb,chij->cbh/dot_general | solution.py:78
  627.6 13.2 %fusion.265 = f32[8,2,128,6]{2,3,1,0:T(8,128)S(1)} fusion(f32[8,2,128,6]{2,3,1,0:T(8,128)S(1)} %get-tuple-element.950, s32[]{:T(128)S(6)} %copy.200, s32[64,512]{1,0:T(8,128)S(1)} %dynamic-slice_bitcast_fusion.7, f32[1,2,6,64,512]{4,3,0,2,1:T(8,128)S(1)} %constant_dynamic-slice_fusion.3), kind=kOutput, calls=%fused_computation.15.clone.1 | convolution fusion | flops 608174080 | bytes 1712132 | tf_op jit(solution)/shard_map/while/body/eval_jaxpr/ijb,chij->cbh/dot_general | solution.py:78
  643.2 13.2 %fusion.265 = f32[8,2,128,6]{2,3,1,0:T(8,128)S(1)} fusion(f32[8,2,128,6]{2,3,1,0:T(8,128)S(1)} %get-tuple-element.950, s32[]{:T(128)S(6)} %copy.200, s32[64,512]{1,0:T(8,128)S(1)} %dynamic-slice_bitcast_fusion.7, f32[1,2,6,64,512]{4,3,0,2,1:T(8,128)S(1)} %constant_dynamic-slice_fusion.3), kind=kOutput, calls=%fused_computation.15.clone.1 | convolution fusion | flops 608174080 | bytes 1712132 | tf_op jit(solution)/shard_map/while/body/eval_jaxpr/ijb,chij->cbh/dot_general | solution.py:78
  658.9 13.2 %fusion.265 = f32[8,2,128,6]{2,3,1,0:T(8,128)S(1)} fusion(f32[8,2,128,6]{2,3,1,0:T(8,128)S(1)} %get-tuple-element.950, s32[]{:T(128)S(6)} %copy.200, s32[64,512]{1,0:T(8,128)S(1)} %dynamic-slice_bitcast_fusion.7, f32[1,2,6,64,512]{4,3,0,2,1:T(8,128)S(1)} %constant_dynamic-slice_fusion.3), kind=kOutput, calls=%fused_computation.15.clone.1 | convolution fusion | flops 608174080 | bytes 1712132 | tf_op jit(solution)/shard_map/while/body/eval_jaxpr/ijb,chij->cbh/dot_general | solution.py:78
  674.6 13.2 %fusion.265 = f32[8,2,128,6]{2,3,1,0:T(8,128)S(1)} fusion(f32[8,2,128,6]{2,3,1,0:T(8,128)S(1)} %get-tuple-element.950, s32[]{:T(128)S(6)} %copy.200, s32[64,512]{1,0:T(8,128)S(1)} %dynamic-slice_bitcast_fusion.7, f32[1,2,6,64,512]{4,3,0,2,1:T(8,128)S(1)} %constant_dynamic-slice_fusion.3), kind=kOutput, calls=%fused_computation.15.clone.1 | convolution fusion | flops 608174080 | bytes 1712132 | tf_op jit(solution)/shard_map/while/body/eval_jaxpr/ijb,chij->cbh/dot_general | solution.py:78
  690.3 13.2 %fusion.265 = f32[8,2,128,6]{2,3,1,0:T(8,128)S(1)} fusion(f32[8,2,128,6]{2,3,1,0:T(8,128)S(1)} %get-tuple-element.950, s32[]{:T(128)S(6)} %copy.200, s32[64,512]{1,0:T(8,128)S(1)} %dynamic-slice_bitcast_fusion.7, f32[1,2,6,64,512]{4,3,0,2,1:T(8,128)S(1)} %constant_dynamic-slice_fusion.3), kind=kOutput, calls=%fused_computation.15.clone.1 | convolution fusion | flops 608174080 | bytes 1712132 | tf_op jit(solution)/shard_map/while/body/eval_jaxpr/ijb,chij->cbh/dot_general | solution.py:78
  706.0 13.2 %fusion.265 = f32[8,2,128,6]{2,3,1,0:T(8,128)S(1)} fusion(f32[8,2,128,6]{2,3,1,0:T(8,128)S(1)} %get-tuple-element.950, s32[]{:T(128)S(6)} %copy.200, s32[64,512]{1,0:T(8,128)S(1)} %dynamic-slice_bitcast_fusion.7, f32[1,2,6,64,512]{4,3,0,2,1:T(8,128)S(1)} %constant_dynamic-slice_fusion.3), kind=kOutput, calls=%fused_computation.15.clone.1 | convolution fusion | flops 608174080 | bytes 1712132 | tf_op jit(solution)/shard_map/while/body/eval_jaxpr/ijb,chij->cbh/dot_general | solution.py:78
  721.7 13.2 %fusion.265 = f32[8,2,128,6]{2,3,1,0:T(8,128)S(1)} fusion(f32[8,2,128,6]{2,3,1,0:T(8,128)S(1)} %get-tuple-element.950, s32[]{:T(128)S(6)} %copy.200, s32[64,512]{1,0:T(8,128)S(1)} %dynamic-slice_bitcast_fusion.7, f32[1,2,6,64,512]{4,3,0,2,1:T(8,128)S(1)} %constant_dynamic-slice_fusion.3), kind=kOutput, calls=%fused_computation.15.clone.1 | convolution fusion | flops 608174080 | bytes 1712132 | tf_op jit(solution)/shard_map/while/body/eval_jaxpr/ijb,chij->cbh/dot_general | solution.py:78
  734.9 77.5 %all-reduce.1 = (f32[2,384]{1,0:T(2,128)}, f32[256,6]{0,1:T(8,128)}, f32[1536]{0:T(1024)}) all-reduce(f32[2,384]{1,0:T(2,128)S(1)} %pad_maximum_fusion, f32[256,6]{0,1:T(8,128)S(1)} %bitcast.336, f32[1536]{0:T(1024)S(1)} %copy-done.50), channel_id=1, replica_groups=mesh['dp'=16,'tensor'=2] {'dp'}, use_global_device_ids=true, to_apply=%region_34.35 | all-reduce | flops 3840 | bytes 30720 | tf_op jit(solution)/shard_map/psum | solution.py:322
  815.3 134.3 %all-reduce.5.cloned.1.call-done = (f32[768,3,384]{0,2,1:T(8,128)}, f32[384,768]{1,0:T(8,128)}, f32[768,1536]{1,0:T(8,128)}, f32[1536,768]{1,0:T(8,128)}) async-done(((f32[768,3,384]{0,2,1:T(8,128)}, f32[384,768]{1,0:T(8,128)}, f32[768,1536]{1,0:T(8,128)}, f32[1536,768]{1,0:T(8,128)}), (f32[768,3,384]{0,2,1:T(8,128)}, f32[384,768]{1,0:T(8,128)}, f32[768,1536]{1,0:T(8,128)}, ...) | async-done | bytes 14155792 | tf_op jit(solution)/shard_map/psum | solution.py:322
  (355 shorter events, 233.8 us)
Async XLA Ops:
  7.2 225.7 %copy-start = (bf16[768,1536]{1,0:T(8,128)(2,1)S(1)}, bf16[768,1536]{1,0:T(8,128)(2,1)}, u32[]{:S(2)}) copy-start(bf16[768,1536]{1,0:T(8,128)(2,1)} %param.36) | copy-start | bytes 7077892
  7.2 129.3 %all-gather.11.cloned.1.call-start = ((), (), s32[]{:S(2)}) async-start(), calls=%async_computation.10 | async-start | bytes 2359296 | tf_op jit(solution)/shard_map/all_gather | solution.py:180
  11.3 206.2 %reduce-scatter.11.cloned.1.call-start = ((), (), s32[]{:S(2)}) async-start(), calls=%async_computation.11 | async-start | bytes 4718592 | tf_op jit(solution)/shard_map/reduce_scatter | solution.py:190
  119.0 17.5 %copy-start.49 = (f32[2,384]{1,0:T(2,128)S(1)}, f32[2,384]{1,0:T(2,128)}, u32[]{:S(2)}) copy-start(f32[2,384]{1,0:T(2,128)} %param.30) | copy-start | bytes 9220
  149.5 14.0 %copy-start.33 = (s32[2,512]{1,0:T(2,128)S(1)}, s32[2,512]{1,0:T(2,128)}, u32[]{:S(2)}) copy-start(s32[2,512]{1,0:T(2,128)} %param.44) | copy-start | bytes 12292
  149.5 14.0 %copy-start.58 = (s32[2]{0:T(128)S(1)}, s32[2]{0:T(128)}, u32[]{:S(2)}) copy-start(s32[2]{0:T(128)} %param.43) | copy-start | bytes 28
  196.7 7.1 copy-start.6
  196.7 7.1 copy-start.34
  199.1 18.4 %copy-start.36 = (f32[768]{0:T(1024)S(1)}, f32[768]{0:T(1024)}, u32[]{:S(2)}) copy-start(f32[768]{0:T(1024)} %param.33) | copy-start | bytes 9220
  203.7 16.9 %copy-start.38 = (f32[768]{0:T(1024)S(1)}, f32[768]{0:T(1024)}, u32[]{:S(2)}) copy-start(f32[768]{0:T(1024)} %param.35) | copy-start | bytes 9220
  203.7 16.9 %copy-start.39 = (f32[768]{0:T(1024)S(1)}, f32[768]{0:T(1024)}, u32[]{:S(2)}) copy-start(f32[768]{0:T(1024)} %param.34) | copy-start | bytes 9220
  203.8 29.2 %copy-start.57 = (f32[1536]{0:T(1024)S(1)}, f32[1536]{0:T(1024)}, u32[]{:S(2)}) copy-start(f32[1536]{0:T(1024)} %param.37) | copy-start | bytes 18436
  203.8 29.1 %all-gather.13.cloned.1.call-start = ((), (), s32[]{:S(2)}) async-start(), calls=%async_computation.12 | async-start | bytes 2359296 | tf_op jit(solution)/shard_map/all_gather | solution.py:199
  221.8 34.9 %all-gather.7.cloned.1.call-start = ((), (), s32[]{:S(2)}) async-start(), calls=%async_computation.6 | async-start | bytes 2359296 | tf_op jit(solution)/shard_map/all_gather | solution.py:180
  222.4 60.5 %reduce-scatter.13.cloned.1.call-start = ((), (), s32[]{:S(2)}) async-start(), calls=%async_computation.13 | async-start | bytes 2359296 | tf_op jit(solution)/shard_map/reduce_scatter | solution.py:202
  232.9 20.0 %copy-start.53 = (bf16[1536,768]{1,0:T(8,128)(2,1)S(1)}, bf16[1536,768]{1,0:T(8,128)(2,1)}, u32[]{:S(2)}) copy-start(bf16[1536,768]{1,0:T(8,128)(2,1)} %param.38) | copy-start | bytes 7077892
  256.6 78.0 %all-gather.15.cloned.1.call-start = ((), (), s32[]{:S(2)}) async-start(), calls=%async_computation.14 | async-start | bytes 2359296 | tf_op jit(solution)/shard_map/all_gather | solution.py:268
  269.8 13.0 %copy-start.42 = (f32[768]{0:T(1024)S(1)}, f32[768]{0:T(1024)}, u32[]{:S(2)}) copy-start(f32[768]{0:T(1024)} %param.39) | copy-start | bytes 9220
  277.5 8.0 copy-start.40
  288.7 62.4 %reduce-scatter.7.cloned.1.call-start = ((), (), s32[]{:S(2)}) async-start(), calls=%async_computation.7 | async-start | bytes 4718592 | tf_op jit(solution)/shard_map/reduce_scatter | solution.py:190
  334.5 26.8 %reduce-scatter.15.cloned.1.call-start = ((), (), s32[]{:S(2)}) async-start(), calls=%async_computation.15 | async-start | bytes 2359296 | tf_op jit(solution)/shard_map/reduce_scatter | solution.py:275
  350.9 26.2 %all-gather.9.cloned.1.call-start = ((), (), s32[]{:S(2)}) async-start(), calls=%async_computation.8 | async-start | bytes 2359296 | tf_op jit(solution)/shard_map/all_gather | solution.py:199
  365.9 41.8 %reduce-scatter.9.cloned.1.call-start = ((), (), s32[]{:S(2)}) async-start(), calls=%async_computation.9 | async-start | bytes 2359296 | tf_op jit(solution)/shard_map/reduce_scatter | solution.py:202
  397.4 27.5 %all-gather.17.cloned.1.call-start = ((), (), s32[]{:S(2)}) async-start(), calls=%async_computation.16 | async-start | bytes 2359296 | tf_op jit(solution)/shard_map/all_gather | solution.py:285
  413.7 398.7 %reduce-scatter.17.cloned.1.call-start = ((), (), s32[]{:S(2)}) async-start(), calls=%async_computation.17 | async-start | bytes 2359296 | tf_op jit(solution)/shard_map/reduce_scatter | solution.py:316
  414.1 18.3 %copy-start.7 = (bf16[2,512,6,64]{1,3,2,0:T(8,128)(2,1)S(1)}, bf16[2,512,6,64]{1,3,2,0:T(8,128)(2,1)}, u32[]{:S(2)}) copy-start(bf16[2,512,6,64]{1,3,2,0:T(8,128)(2,1)} %copy-done.6) | copy-start | bytes 2359300
  414.1 18.3 %copy-start.8 = (bf16[2,512,6,64]{1,3,2,0:T(8,128)(2,1)S(1)}, bf16[2,512,6,64]{1,3,2,0:T(8,128)(2,1)}, u32[]{:S(2)}) copy-start(bf16[2,512,6,64]{1,3,2,0:T(8,128)(2,1)} %get-tuple-element.997) | copy-start | bytes 2359300
  414.1 18.3 %copy-start.35 = (f32[2,6,512,1]{2,1,3,0:T(8,128)S(1)}, f32[2,6,512,1]{2,1,3,0:T(8,128)}, u32[]{:S(2)}) copy-start(f32[2,6,512,1]{2,1,3,0:T(8,128)} %copy-done.34) | copy-start | bytes 73732
  435.9 8.5 copy-start.3
  435.9 11.1 %copy-start.14 = (bf16[2,512,6,64]{1,3,2,0:T(8,128)(2,1)S(1)}, bf16[2,512,6,64]{1,3,2,0:T(8,128)(2,1)}, u32[]{:S(2)}) copy-start(bf16[2,512,6,64]{1,3,2,0:T(8,128)(2,1)} %get-tuple-element.918) | copy-start | bytes 2359300 | tf_op jit(solution)/shard_map/while
  448.1 11.3 %copy-start.15 = (bf16[2,512,6,64]{1,3,2,0:T(8,128)(2,1)}, bf16[2,512,6,64]{1,3,2,0:T(8,128)(2,1)S(1)}, u32[]{:S(2)}) copy-start(bf16[2,512,6,64]{1,3,2,0:T(8,128)(2,1)S(1)} %fusion.277) | copy-start | bytes 2359300 | tf_op jit(solution)/shard_map/while
  477.2 8.5 copy-start.3
  477.2 11.1 %copy-start.14 = (bf16[2,512,6,64]{1,3,2,0:T(8,128)(2,1)S(1)}, bf16[2,512,6,64]{1,3,2,0:T(8,128)(2,1)}, u32[]{:S(2)}) copy-start(bf16[2,512,6,64]{1,3,2,0:T(8,128)(2,1)} %get-tuple-element.918) | copy-start | bytes 2359300 | tf_op jit(solution)/shard_map/while
  489.4 11.3 %copy-start.15 = (bf16[2,512,6,64]{1,3,2,0:T(8,128)(2,1)}, bf16[2,512,6,64]{1,3,2,0:T(8,128)(2,1)S(1)}, u32[]{:S(2)}) copy-start(bf16[2,512,6,64]{1,3,2,0:T(8,128)(2,1)S(1)} %fusion.277) | copy-start | bytes 2359300 | tf_op jit(solution)/shard_map/while
  531.0 7.4 copy-start.28
  531.0 418.7 %all-reduce.5.cloned.1.call-start = ((), (), s32[]{:S(2)}) async-start(), calls=%async_computation.18 | async-start | bytes 28311552 | tf_op jit(solution)/shard_map/psum | solution.py:322
  531.0 7.4 copy-start.23
  549.3 45.2 %copy-start.51 = (f32[512]{0:T(512)S(1)}, f32[512]{0:T(512)}, u32[]{:S(2)}) copy-start(f32[512]{0:T(512)} %get-tuple-element.576) | copy-start | bytes 6148
  549.3 45.2 %copy-start.11 = (f32[512,768]{1,0:T(8,128)S(1)}, f32[512,768]{1,0:T(8,128)}, u32[]{:S(2)}) copy-start(f32[512,768]{1,0:T(8,128)} %get-tuple-element.577) | copy-start | bytes 4718596
  549.3 45.5 %copy-start.41 = (f32[768]{0:T(1024)S(1)}, f32[768]{0:T(1024)}, u32[]{:S(2)}) copy-start(f32[768]{0:T(1024)} %param.40) | copy-start | bytes 9220
  549.3 45.5 %copy-start.52 = (f32[768]{0:T(1024)S(1)}, f32[768]{0:T(1024)}, u32[]{:S(2)}) copy-start(f32[768]{0:T(1024)} %param.41) | copy-start | bytes 9220
  596.0 12.8 %copy-start.16 = (bf16[2,512,6,64]{1,3,2,0:T(8,128)(2,1)S(1)}, bf16[2,512,6,64]{1,3,2,0:T(8,128)(2,1)}, u32[]{:S(2)}) copy-start(bf16[2,512,6,64]{1,3,2,0:T(8,128)(2,1)} %get-tuple-element.257) | copy-start | bytes 2359300
  596.0 13.0 %copy-start.19 = (bf16[2,512,6,64]{1,3,2,0:T(8,128)(2,1)S(1)}, bf16[2,512,6,64]{1,3,2,0:T(8,128)(2,1)}, u32[]{:S(2)}) copy-start(bf16[2,512,6,64]{1,3,2,0:T(8,128)(2,1)} %get-tuple-element.255) | copy-start | bytes 2359300
  609.4 125.5 %copy-start.50 = (f32[1536]{0:T(1024)S(1)}, f32[1536]{0:T(1024)}, u32[]{:S(2)}) copy-start(f32[1536]{0:T(1024)} %get-tuple-element.556) | copy-start | bytes 18436
  949.7 5.3 copy-start.29
  954.9 6.5 slice-start.2
  955.9 5.5 slice-start.3
  955.9 7.7 copy-start.1
  (42 other events, 98.2 us)
Sparse Core Ops, SparseCore 0:
  11.4 12.5 all-gather.10
  203.9 13.6 reduce-scatter.10
  221.9 10.9 all-gather.12
  234.4 10.9 all-gather.6
  256.7 10.2 reduce-scatter.12
  288.9 11.0 all-gather.14
  334.6 12.1 reduce-scatter.6
  351.0 10.3 reduce-scatter.14
  366.0 10.9 all-gather.8
  397.5 10.1 reduce-scatter.8
  413.8 10.9 all-gather.16
  531.1 10.2 reduce-scatter.16
  549.5 400.1 all-reduce.4
where the time goes:
time: 981 us; the launch traced here: 970 us
  matrix products  379 us (39%)
  waiting for transfers between devices  198 us (20%)
  local copies, waits for them, and re-layouts  158 us (16%)
  blocking collectives  122 us (12%)
  other arithmetic  84.7 us (9%)
  between operations  14.7 us (1%)
  loops' own time  13 us (1%)
    psum x1, waiting for transfers between devices, on_device(): lax.psum((grad_weight_mixed, grad_qv, grad_table, grad_out, grad_up, grad...  134 us
    dot_general x8, matrix products, fold_bucket_rows(): jnp.einsum('ijb,chij->cbh', onehot, grads, precision=lax.Precision.HIGHEST)  105 us
    dot_general x8, matrix products, position_bucket_rows(): jnp.einsum('ijb,cbh->chij', onehot, halves, precision=lax.Precision.HIGHEST)  100 us
    psum x1, blocking collectives, on_device(): lax.psum((grad_weight_mixed, grad_qv, grad_table, grad_out, grad_up, grad...  77.5 us
    psum x1, blocking collectives, on_device(): lax.psum((grad_out_bias, grad_gain_one, grad_shift_one, grad_down_bias, g...  44.5 us
    dot_general x6, matrix products, pair_scores(): jnp.einsum('ihd,jhd->hij', query, keys, preferred_element_type=jnp.float32)  42.4 us
    while x7, local copies, waits for them, and re-layouts, forward(): lax.map(partial(pair_forward, terms), (query.reshape(shape), keys.reshape...  28.4 us
    unnamed x115, local copies, waits for them, and re-layouts  28 us
  transfers between devices with their start and end apart: 13, of which 7 were waited for; matrix products, arithmetic and copies ran while one was open for 40% of the time, Pallas kernels for 0%

commit v1 on v0

v1 whole, which is shorter than its diff:
```python
import functools
import math

import jax
import jax.numpy as jnp
from jax import lax
from jax.experimental import pallas as pl
from jax.experimental.pallas import tpu as pltpu
from jax.sharding import PartitionSpec as P

EPSILON = 1e-05
FAR_BELOW = -1000000000.0
MESH = pl.DeviceIdType.MESH
F32 = jnp.float32
BF16 = jnp.bfloat16
LANES = 128
NT = (((1,), (1,)), ((), ()))
TN = (((0,), (0,)), ((), ()))
VMEM_LIMIT = 62 * 2**20


def dot(left, right, dims=None):
    if dims is None:
        return jnp.dot(left, right, preferred_element_type=F32)
    return lax.dot_general(left, right, dims, preferred_element_type=F32)


def other_core():
    return {"tensor": 1 - lax.axis_index("tensor")}


def row(ref):
    return ref[...].reshape(1, ref.shape[-1])


def fold8(block):
    return jnp.sum(block.reshape(block.shape[0] // 8, 8, block.shape[1]), axis=0)


def pack_tables(tab, packed):
    step = jnp.maximum(jnp.max(jnp.abs(tab[...])), 1e-30) / 32000.0
    inverse = 1.0 / step
    heads = tab.shape[1]
    for core in range(2):
        for pair in range(heads // 2):
            high = tab[core, 2 * pair : 2 * pair + 1, :] * inverse
            low = jnp.round(tab[core, 2 * pair + 1 : 2 * pair + 2, :] * inverse)
            high = jnp.round(high - low * (1 / 65536.0))
            both = high.astype(jnp.int32) * 65536 + low.astype(jnp.int32)
            packed[core * (heads // 2) + pair] = jnp.broadcast_to(both, packed.shape[1:])
    return step


def attend_pair(pair, q, k, vt, packed, bucket, valid, length, step, expo, heads_t, recip):
    seq = q.shape[0]
    cols = pl.ds(pl.multiple_of(pair * LANES, LANES), LANES)
    keys = k[:, cols]
    queries = q[:, cols]
    lane = lax.broadcasted_iota(jnp.int32, (seq, LANES), 1)
    in_query = lax.broadcasted_iota(jnp.int32, (seq, LANES), 0) < length
    terms = packed[pair, 0:1, :]
    near = jnp.broadcast_to(terms[:, :LANES], (seq, LANES))
    far = jnp.broadcast_to(terms[:, LANES:], (seq, LANES))
    same = jnp.where(in_query, far, near)
    swap = jnp.where(in_query, near, far)
    pieces = ([], [])
    for start in range(0, seq, LANES):
        index = bucket[:, start : start + LANES]
        got = jnp.take_along_axis(same, index, axis=1, mode="promise_in_bounds")
        if start == 0:
            turned = jnp.take_along_axis(swap, index, axis=1, mode="promise_in_bounds")
            got = jnp.where(lane < length, turned, got)
        pieces[0].append(got.astype(F32) * (step * (1 / 65536.0)))
        pieces[1].append(jnp.left_shift(got, 16).astype(F32) * (step * (1 / 65536.0)))
    first = lane < LANES // 2
    real = jnp.concatenate([valid[...] > 0] * (seq // LANES), axis=1)
    for side in range(2):
        mine = first if side == 0 else jnp.logical_not(first)
        scores = dot(jnp.where(mine, keys, jnp.zeros_like(keys)), queries, NT)
        scores = scores + jnp.concatenate(pieces[side], axis=1)
        scores = jnp.where(real, scores, FAR_BELOW)
        highest = jnp.max(scores, axis=0, keepdims=True)
        weights = jnp.exp(scores - highest).astype(BF16)
        expo[2 * pair + side] = weights
        rows = pl.ds(pl.multiple_of(pair * LANES + side * 64, 64), 64)
        values = jnp.concatenate([vt[rows, :], jnp.ones((16, seq), BF16)], axis=0)
        got = dot(values, weights)
        inverse = 1.0 / got[64:65]
        heads_t[rows, :] = (got[:64] * inverse).astype(BF16)
        recip[2 * pair + side] = jnp.broadcast_to(inverse, recip.shape[1:])


def forward_kernel(
    tokens_h,
    qkvw_h,
    qvb_h,
    tab_h,
    outw_h,
    upw_h,
    upb_h,
    downw_h,
    upstream_h,
    outb,
    gain1,
    shift1,
    downb,
    gain2,
    shift2,
    bucket,
    length,
    mask,
    out_h,
    gsec_h,
    gbr_h,
    act_h,
    slope_h,
    first_h,
    normed1_h,
    inverse1_h,
    heads_h,
    q_h,
    k_h,
    v_h,
    expo_h,
    recip_h,
    qkvw_o,
    outw_o,
    upw_o,
    downw_o,
    sums,
    tokens,
    qkvw,
    qvb,
    tab,
    outw,
    upw,
    upb,
    downw,
    upstream,
    packed,
    valid,
    q,
    k,
    v,
    vt,
    heads_t,
    expo,
    recip,
    wide,
    first32,
    normed1,
    inverse1,
    first16,
    act,
    slope,
    gsec,
    gbr,
    out,
    in_sem,
    out_sem,
    send_sem,
    recv_sem,
):
    seq, width = tokens.shape
    inner = qkvw.shape[3]
    half_units = upw.shape[2]
    pairs = inner // LANES
    barrier = pltpu.get_barrier_semaphore()
    pl.semaphore_signal(barrier, inc=1, device_id=other_core(), device_id_type=MESH)

    loads = []
    for number, (source, target) in enumerate(
        (
            (tokens_h, tokens),
            (qkvw_h, qkvw.at[0]),
            (qvb_h, qvb.at[0]),
            (tab_h, tab.at[0]),
            (outw_h, outw.at[0]),
            (upw_h, upw.at[0]),
            (upb_h, upb.at[0]),
            (downw_h, downw.at[0]),
            (upstream_h, upstream),
        )
    ):
        copy = pltpu.make_async_copy(source, target, in_sem.at[number])
        copy.start()
        loads.append(copy)

    pl.semaphore_wait(barrier, 1)
    sends = []
    for number, (source, target) in enumerate(
        (
            (qkvw_h, qkvw.at[1]),
            (qvb_h, qvb.at[1]),
            (tab_h, tab.at[1]),
            (outw_h, outw.at[1]),
            (upw_h, upw.at[1]),
            (upb_h, upb.at[1]),
            (downw_h, downw.at[1]),
        )
    ):
        copy = pltpu.make_async_remote_copy(
            src_ref=source,
            dst_ref=target,
            send_sem=send_sem.at[number],
            recv_sem=recv_sem.at[number],
            device_id=other_core(),
            device_id_type=MESH,
        )
        copy.start()
        sends.append(copy)

    stores = []

    def store(source, target):
        copy = pltpu.make_async_copy(source, target, out_sem.at[len(stores)])
        copy.start()
        stores.append(copy)

    me = lax.axis_index("tensor")
    span = length[me]
    mine = mask[pl.ds(me, 1), :].astype(F32)
    valid[...] = jnp.transpose(jnp.broadcast_to(mine, (LANES, seq)))

    def mix(core):
        rows = tokens[...]
        cols = slice(core * inner, (core + 1) * inner)
        query = dot(rows, qkvw[core, 0])
        q[:, cols] = ((query + qvb[core, 0:1, :]) * 0.125).astype(BF16)
        k[:, cols] = dot(rows, qkvw[core, 1]).astype(BF16)
        value = (dot(rows, qkvw[core, 2]) + qvb[core, 1:2, :]).astype(BF16)
        v[:, cols] = value
        vt[cols, :] = jnp.transpose(value)

    loads[0].wait()
    loads[1].wait()
    loads[2].wait()
    mix(0)
    loads[3].wait()
    sends[0].wait_recv()
    sends[1].wait_recv()
    sends[2].wait_recv()
    mix(1)
    step = pack_tables(tab, packed)
    store(q, q_h)
    store(k, k_h)
    store(v, v_h)
    store(qkvw.at[1], qkvw_o)

    def attend(pair, carry):
        attend_pair(pair, q, k, vt, packed, bucket, valid, span, step, expo, heads_t, recip)
        return carry

    lax.fori_loop(0, 2 * pairs, attend, 0)
    store(expo, expo_h)
    store(recip, recip_h)
    store(heads_t, heads_h)

    loads[4].wait()
    sends[3].wait_recv()
    store(outw.at[1], outw_o)
    lower = jnp.transpose(heads_t[...])

    def project(tile, carry):
        cols = pl.ds(pl.multiple_of(tile * 256, 256), 256)
        wide[:, cols] = dot(lower[:, :inner], outw[0, :, cols]) + dot(
            lower[:, inner:], outw[1, :, cols]
        )
        return carry

    lax.fori_loop(0, width // 256, project, 0)
    block = 128

    def norm_one(number, carry):
        rows = pl.ds(pl.multiple_of(number * block, block), block)
        value = wide[rows, :] + row(outb) + tokens[rows, :].astype(F32)
        center = value - jnp.mean(value, axis=-1, keepdims=True)
        inverse = lax.rsqrt(jnp.mean(center * center, axis=-1, keepdims=True) + EPSILON)
        normed = center * inverse
        result = normed * row(gain1) + row(shift1)
        normed1[rows, :] = normed
        inverse1[rows, :] = jnp.broadcast_to(inverse, (block, LANES))
        first32[rows, :] = result
        first16[rows, :] = result.astype(BF16)
        return carry

    lax.fori_loop(0, seq // block, norm_one, 0)
    store(first16, first_h)
    store(normed1, normed1_h)
    store(inverse1, inverse1_h)

    for core in range(2):
        if core == 0:
            loads[5].wait()
            loads[6].wait()
        else:
            sends[4].wait_recv()
            sends[5].wait_recv()
            store(upw.at[1], upw_o)

        def expand(tile, carry, core=core):
            cols = pl.ds(pl.multiple_of(tile * 256, 256), 256)
            here = pl.ds(pl.multiple_of(core * half_units + tile * 256, 256), 256)
            hidden = dot(first16[...], upw[core, :, cols]) + upb[core, :, cols]
            chance = 0.5 * (1.0 + lax.erf(hidden * math.sqrt(0.5)))
            density = jnp.exp(hidden * hidden * -0.5) * (1.0 / math.sqrt(2.0 * math.pi))
            act[:, here] = (hidden * chance).astype(BF16)
            slope[:, here] = (chance + hidden * density).astype(BF16)
            return carry

        lax.fori_loop(0, half_units // 256, expand, 0)
    store(act, act_h)
    store(slope, slope_h)
    loads[7].wait()
    sends[6].wait_recv()
    store(downw.at[1], downw_o)

    def reduce_units(tile, carry):
        cols = pl.ds(pl.multiple_of(tile * 256, 256), 256)
        wide[:, cols] = dot(act[:, :half_units], downw[0, :, cols]) + dot(
            act[:, half_units:], downw[1, :, cols]
        )
        return carry

    lax.fori_loop(0, width // 256, reduce_units, 0)
    loads[8].wait()

    def norm_two(number, carry):
        rows = pl.ds(pl.multiple_of(number * block, block), block)
        value = wide[rows, :] + row(downb) + first32[rows, :]
        center = value - jnp.mean(value, axis=-1, keepdims=True)
        inverse = lax.rsqrt(jnp.mean(center * center, axis=-1, keepdims=True) + EPSILON)
        normed = center * inverse
        out[rows, :] = (normed * row(gain2) + row(shift2)).astype(BF16)
        grad = upstream[rows, :].astype(F32)
        scaled = grad * row(gain2)
        back = inverse * (
            scaled
            - jnp.mean(scaled, axis=-1, keepdims=True)
            - normed * jnp.mean(scaled * normed, axis=-1, keepdims=True)
        )
        gsec[rows, :] = back
        gbr[rows, :] = back.astype(BF16)
        return (
            carry[0] + fold8(grad * normed),
            carry[1] + fold8(grad),
            carry[2] + fold8(back),
        )

    zero = jnp.zeros((8, width), F32)
    totals = lax.fori_loop(0, seq // block, norm_two, (zero, zero, zero))
    for number, total in enumerate(totals):
        sums[number : number + 1, :] = jnp.sum(total, axis=0, keepdims=True)
    sums[3:, :] = jnp.zeros((5, width), F32)
    store(out, out_h)
    store(gsec, gsec_h)
    store(gbr, gbr_h)
    for copy in stores:
        copy.wait()
    for copy in sends:
        copy.wait_send()


def forward(
    tokens,
    qkvw,
    qvb,
    tab,
    outw,
    outb,
    gain1,
    shift1,
    upw,
    upb,
    downw,
    downb,
    gain2,
    shift2,
    bucket,
    length,
    mask,
    upstream,
):
    seq, width = tokens.shape
    inner = qkvw.shape[2]
    units = upw.shape[1]
    heads = 2 * tab.shape[0]
    shape = jax.ShapeDtypeStruct
    here = pl.BlockSpec(memory_space=pltpu.VMEM)
    away = pl.BlockSpec(memory_space=pl.ANY)
    scalar = pl.BlockSpec(memory_space=pltpu.SMEM)
    out_shape = (
        shape((seq, width), BF16),
        shape((seq, width), F32),
        shape((seq, width), BF16),
        shape((seq, 2 * units), BF16),
        shape((seq, 2 * units), BF16),
        shape((seq, width), BF16),
        shape((seq, width), F32),
        shape((seq, LANES), F32),
        shape((2 * inner, seq), BF16),
        shape((seq, 2 * inner), BF16),
        shape((seq, 2 * inner), BF16),
        shape((seq, 2 * inner), BF16),
        shape((heads, seq, seq), BF16),
        shape((heads, 8, seq), F32),
        shape(qkvw.shape, BF16),
        shape(outw.shape, BF16),
        shape(upw.shape, BF16),
        shape(downw.shape, BF16),
        shape((8, width), F32),
    )
    scratch = [
        pltpu.VMEM((seq, width), BF16),
        pltpu.VMEM((2,) + qkvw.shape, BF16),
        pltpu.VMEM((2,) + qvb.shape, F32),
        pltpu.VMEM((2,) + tab.shape, F32),
        pltpu.VMEM((2,) + outw.shape, BF16),
        pltpu.VMEM((2,) + upw.shape, BF16),
        pltpu.VMEM((2,) + upb.shape, F32),
        pltpu.VMEM((2,) + downw.shape, BF16),
        pltpu.VMEM((seq, width), BF16),
        pltpu.VMEM((heads // 2, 8, 2 * LANES), jnp.int32),
        pltpu.VMEM((seq, LANES), F32),
        pltpu.VMEM((seq, 2 * inner), BF16),
        pltpu.VMEM((seq, 2 * inner), BF16),
        pltpu.VMEM((seq, 2 * inner), BF16),
        pltpu.VMEM((2 * inner, seq), BF16),
        pltpu.VMEM((2 * inner, seq), BF16),
        pltpu.VMEM((heads, seq, seq), BF16),
        pltpu.VMEM((heads, 8, seq), F32),
        pltpu.VMEM((seq, width), F32),
        pltpu.VMEM((seq, width), F32),
        pltpu.VMEM((seq, width), F32),
        pltpu.VMEM((seq, LANES), F32),
        pltpu.VMEM((seq, width), BF16),
        pltpu.VMEM((seq, 2 * units), BF16),
        pltpu.VMEM((seq, 2 * units), BF16),
        pltpu.VMEM((seq, width), F32),
        pltpu.VMEM((seq, width), BF16),
        pltpu.VMEM((seq, width), BF16),
        pltpu.SemaphoreType.DMA((9,)),
        pltpu.SemaphoreType.DMA((20,)),
        pltpu.SemaphoreType.DMA((7,)),
        pltpu.SemaphoreType.DMA((7,)),
    ]
    return pl.pallas_call(
        forward_kernel,
        out_shape=out_shape,
        in_specs=[away] * 9 + [here] * 7 + [scalar, here],
        out_specs=(away,) * 18 + (here,),
        scratch_shapes=scratch,
        compiler_params=pltpu.CompilerParams(
            collective_id=0, has_side_effects=True, vmem_limit_bytes=VMEM_LIMIT
        ),
    )(
        tokens,
        qkvw,
        qvb,
        tab,
        outw,
        upw,
        upb,
        downw,
        upstream,
        outb,
        gain1,
        shift1,
        downb,
        gain2,
        shift2,
        bucket,
        length,
        mask,
    )


def dp_side(bit):
    return lax.rem(lax.axis_index("dp") // (1 << bit), 2)


def dp_partner(bit):
    return {"dp": lax.axis_index("dp") + (1 - 2 * dp_side(bit)) * (1 << bit)}


def flat_rows(start, size):
    return pl.ds(pl.multiple_of(start, 16), size)


class Kit:
    def __init__(self, acc, landing, result, send_sem, recv_sem, local_sem):
        self.acc, self.landing, self.result = acc, landing, result
        self.send_sem, self.recv_sem, self.local_sem = send_sem, recv_sem, local_sem
        self.used = 0
        self.landed = 0
        self.pieces = []

    def slot(self):
        self.used += 1
        return self.used - 1

    def room(self, size):
        self.landed += size
        return self.landed - size

    def remote(self, slot, source, target, device):
        return pltpu.make_async_remote_copy(
            src_ref=source,
            dst_ref=target,
            send_sem=self.send_sem.at[slot],
            recv_sem=self.recv_sem.at[slot],
            device_id=device,
            device_id_type=MESH,
        )


class Piece:
    def __init__(self, start, length, order, extra, kit):
        self.start, self.length = start, length
        self.bits, self.extra = order, extra
        self.kit = kit
        self.number = len(kit.pieces)
        self.steps = 2 * len(order) + 1
        kit.pieces.append(self)
        self.halving = [
            (kit.slot(), kit.room(length >> (level + 1))) for level in range(len(order))
        ]
        self.crossing = [(kit.slot(), kit.room(length >> len(order))) for _ in extra]
        self.spreading = [kit.slot() for _ in order]
        self.sent = []

    def begin(self, levels):
        at = self.start
        for level in range(levels):
            at = at + dp_side(self.bits[level]) * (self.length >> (level + 1))
        return at

    def halve(self, level):
        kit, bit = self.kit, self.bits[level]
        slot, room = self.halving[level]
        size = self.length >> (level + 1)
        away = self.begin(level) + (1 - dp_side(bit)) * size
        return kit.remote(
            slot,
            kit.acc.at[flat_rows(away, size), :],
            kit.landing.at[pl.ds(room, size), :],
            dp_partner(bit),
        )

    def swap(self, number):
        kit = self.kit
        slot, room = self.crossing[number]
        size = self.length >> len(self.bits)
        return kit.remote(
            slot,
            kit.acc.at[flat_rows(self.begin(len(self.bits)), size), :],
            kit.landing.at[pl.ds(room, size), :],
            dp_partner(self.extra[number]),
        )

    def keep(self):
        kit, levels = self.kit, len(self.bits)
        mine = flat_rows(self.begin(levels), self.length >> levels)
        return pltpu.make_async_copy(
            kit.acc.at[mine, :], kit.result.at[mine, :], kit.local_sem.at[self.number]
        )

    def spread(self, number):
        kit = self.kit
        level = len(self.bits) - number
        mine = flat_rows(self.begin(level), self.length >> level)
        source = kit.acc if number == 0 else kit.result
        return kit.remote(
            self.spreading[number],
            source.at[mine, :],
            kit.result.at[mine, :],
            dp_partner(self.bits[level - 1]),
        )

    def add(self, target, source, size):
        kit = self.kit
        chunk = math.gcd(size, 192)

        def some(number, carry):
            there = flat_rows(target + number * chunk, chunk)
            here = flat_rows(source + number * chunk, chunk)
            total = kit.acc[there, :].astype(F32) + kit.landing[here, :].astype(F32)
            kit.acc[there, :] = total.astype(BF16)
            return carry

        lax.fori_loop(0, size // chunk, some, 0)

    def run(self, step):
        levels = len(self.bits)
        if 0 < step <= levels:
            self.halve(step - 1).wait_recv()
            self.add(self.begin(step), self.halving[step - 1][1], self.length >> step)
        if step < levels:
            self.halve(step).start()
            self.sent.append(functools.partial(self.halve, step))
            return
        if step == levels:
            for number in range(len(self.extra)):
                both = self.swap(number)
                both.start()
                both.wait()
                self.add(self.begin(levels), self.crossing[number][1], self.length >> levels)
            self.keep().start()
        else:
            self.spread(step - levels - 1).wait_recv()
            if step == levels + 1:
                self.keep().wait()
        if step < 2 * levels:
            self.spread(step - levels).start()
            self.sent.append(functools.partial(self.spread, step - levels))

    def finish(self):
        for sent in self.sent:
            sent().wait_send()


class Vectors:
    def __init__(self, parts, landing, result, bits, kit, send_sem, recv_sem):
        self.parts, self.landing, self.result = parts, landing, result
        self.bits = bits
        self.steps = bits + 2
        self.send_sem, self.recv_sem = send_sem, recv_sem
        kit.pieces.append(self)

    def exchange(self, step):
        return pltpu.make_async_remote_copy(
            src_ref=self.parts.at[step],
            dst_ref=self.landing.at[step],
            send_sem=self.send_sem.at[step],
            recv_sem=self.recv_sem.at[step],
            device_id=other_core() if step == 0 else dp_partner(step - 1),
            device_id_type=MESH,
        )

    def run(self, step):
        if step > 0:
            self.exchange(step - 1).wait_recv()
            total = self.parts[max(step - 1, 1)] + self.landing[step - 1]
            if step <= self.bits:
                self.parts[step] = total
            else:
                self.result[...] = total
        if step <= self.bits:
            self.exchange(step).start()

    def finish(self):
        for step in range(self.bits + 1):
            self.exchange(step).wait_send()


def backward_kernel(
    plan,
    bits,
    gbr_h,
    act_h,
    slope_h,
    first_h,
    gsec_h,
    normed1_h,
    inverse1_h,
    heads_h,
    q_h,
    k_h,
    v_h,
    expo_h,
    recip_h,
    qkvw_h,
    outw_h,
    upw_h,
    downw_h,
    qkvw_o,
    outw_o,
    upw_o,
    downw_o,
    tokens_h,
    sums2,
    gain1,
    bucket,
    length,
    result_h,
    gtok_h,
    small,
    acc,
    xsend,
    xrecv,
    landing,
    gbr,
    gsec,
    normed1,
    inverse1,
    heads_t,
    outw,
    gmid16,
    wide,
    q,
    k,
    v,
    recip,
    ups,
    vparts,
    vland,
    in_sem,
    out_sem,
    send_sem,
    recv_sem,
    local_sem,
    xs_sem,
    xr_sem,
    vs_sem,
    vr_sem,
):
    seq, width = gsec.shape
    inner = outw.shape[1]
    units = upw_h.shape[1]
    heads = recip.shape[0]
    levels = min(4, bits)

    barrier = pltpu.get_barrier_semaphore()
    pl.semaphore_signal(barrier, inc=1, device_id=other_core(), device_id_type=MESH)
    for bit in range(bits):
        pl.semaphore_signal(barrier, inc=1, device_id=dp_partner(bit), device_id_type=MESH)

    used = []

    def load(source, target):
        copy = pltpu.make_async_copy(source, target, in_sem.at[len(used)])
        used.append(copy)
        copy.start()
        return copy

    kit = Kit(acc, landing, result_h, send_sem, recv_sem, local_sem)
    orders = {
        "x": tuple(range(levels)),
        "y": ((1, 0) + tuple(range(2, levels)))[:levels] if levels > 1 else tuple(range(levels)),
        "z": tuple(range(2, levels)) + tuple(range(min(2, levels))),
    }
    extra = tuple(range(levels, bits))
    crossed = []

    def cross(start, size, place):
        number = len(crossed)

        def copy():
            return pltpu.make_async_remote_copy(
                src_ref=xsend.at[pl.ds(place, size), :],
                dst_ref=xrecv.at[pl.ds(start, size), :],
                send_sem=xs_sem.at[number],
                recv_sem=xr_sem.at[number],
                device_id=other_core(),
                device_id_type=MESH,
            )

        copy().start()
        crossed.append(copy)

    polls = [0]

    def poll():
        for number, step in plan.get(polls[0], ()):
            kit.pieces[number].run(step)
        polls[0] += 1

    def begin_piece(start, size, order):
        fresh = Piece(start, size, orders[order], extra, kit)
        fresh.run(0)

    def give(place, tile):
        xsend[flat_rows(place, tile.shape[0]), :] = tile.astype(BF16)

    def take(start, tile):
        there = flat_rows(start, tile.shape[0])
        acc[there, :] = (tile + xrecv[there, :].astype(F32)).astype(BF16)

    third = acc.shape[0] // 3
    split = width // inner

    def unit_phase(act, slope, downw, upw, first, first_t):
        l_gbr = load(gbr_h, gbr)
        l_act = [None, load(act_h.at[:, pl.ds(units, units)], act.at[:, pl.ds(units, units)])]
        l_act[0] = load(act_h.at[:, pl.ds(0, units)], act.at[:, pl.ds(0, units)])
        l_down = [None, load(downw_o, downw.at[1])]
        l_slope = load(slope_h, slope)
        l_down[0] = load(downw_h, downw.at[0])
        l_first = load(first_h, first)
        l_up = [load(upw_h, upw.at[0]), load(upw_o, upw.at[1])]
        l_late = [
            load(source, target)
            for source, target in (
                (gsec_h, gsec),
                (normed1_h, normed1),
                (inverse1_h, inverse1),
                (heads_h, heads_t),
                (outw_h, outw.at[0]),
                (outw_o, outw.at[1]),
                (recip_h, recip),
                (q_h, q),
                (k_h, k),
                (v_h, v),
            )
        ]
        pl.semaphore_wait(barrier, 1 + bits)

        tiles = units // 256
        group = tiles // 3
        span = 256 * split
        l_gbr.wait()
        for core in (1, 0):
            l_act[core].wait()
            for part in range(3):
                if core == 0:
                    crossed[part]().wait_recv()

                def down_tile(number, carry, core=core):
                    cols = pl.ds(pl.multiple_of(core * units + number * 256, 256), 256)
                    tile = dot(act[:, cols], gbr[...], TN)
                    for side in range(split):
                        (give if core == 1 else take)(
                            number * span + side * 256,
                            tile[:, side * inner : (side + 1) * inner],
                        )
                    return carry

                lax.fori_loop(part * group, (part + 1) * group, down_tile, 0)
                start = part * group * span
                if core == 1:
                    cross(start, group * span, start)
                else:
                    begin_piece(start, group * span, "xyz"[part])
                    poll()

        l_slope.wait()
        for core in (1, 0):
            l_down[core].wait()
            for part in range(2):

                def slope_tile(number, carry, core=core):
                    here = pl.ds(pl.multiple_of(number * 256, 256), 256)
                    cols = pl.ds(pl.multiple_of(core * units + number * 256, 256), 256)
                    tile = dot(gbr[...], downw[core, here, :], NT) * slope[:, cols].astype(F32)
                    tile = tile.astype(BF16)
                    slope[:, cols] = tile
                    ups[core, :, here] = fold8(tile.astype(F32))
                    return carry

                lax.fori_loop(part * (tiles // 2), (part + 1) * (tiles // 2), slope_tile, 0)
                poll()

        l_first.wait()
        first_t[...] = jnp.transpose(first[...])
        for copy in crossed[:3]:
            copy().wait_send()
        blocks = units // inner
        for core in (1, 0):
            for part in range(2):
                if core == 0:
                    crossed[3 + part]().wait_recv()

                def up_tile(number, carry, core=core):
                    cols = pl.ds(pl.multiple_of(core * units + number * inner, LANES), inner)
                    for top in range(0, width, 256):
                        tile = dot(first_t[top : top + 256, :], slope[:, cols])
                        if core == 1:
                            give(number * width + top, tile)
                        else:
                            take(third + number * width + top, tile)
                    return carry

                lax.fori_loop(part * (blocks // 2), (part + 1) * (blocks // 2), up_tile, 0)
                size = (blocks // 2) * width
                if core == 1:
                    cross(third + part * size, size, part * size)
                else:
                    begin_piece(third + part * size, size, "xy"[part])
                poll()

        l_up[0].wait()
        l_up[1].wait()
        l_late[0].wait()

        def first_tile(number, carry):
            cols = pl.ds(pl.multiple_of(number * 256, 256), 256)
            wide[:, cols] = (
                gsec[:, cols]
                + dot(slope[:, :units], upw[0, cols, :], NT)
                + dot(slope[:, units:], upw[1, cols, :], NT)
            )
            return carry

        lax.fori_loop(0, width // 256, first_tile, 0)
        poll()
        for copy in l_late[1:]:
            copy.wait()

    pl.run_scoped(
        unit_phase,
        pltpu.VMEM((seq, 2 * units), BF16),
        pltpu.VMEM((seq, 2 * units), BF16),
        pltpu.VMEM((2, units, width), BF16),
        pltpu.VMEM((2, width, units), BF16),
        pltpu.VMEM((seq, width), BF16),
        pltpu.VMEM((width, seq), BF16),
    )

    block = 128

    def norm_one(number, carry):
        rows = pl.ds(pl.multiple_of(number * block, block), block)
        grad = wide[rows, :]
        normed = normed1[rows, :]
        scaled = grad * row(gain1)
        back = inverse1[rows, 0:1] * (
            scaled
            - jnp.mean(scaled, axis=-1, keepdims=True)
            - normed * jnp.mean(scaled * normed, axis=-1, keepdims=True)
        )
        wide[rows, :] = back
        gmid16[rows, :] = back.astype(BF16)
        return (
            carry[0] + fold8(back),
            carry[1] + fold8(grad * normed),
            carry[2] + fold8(grad),
        )

    zero = jnp.zeros((8, width), F32)
    totals = lax.fori_loop(0, seq // block, norm_one, (zero, zero, zero))
    both = [jnp.sum(total, axis=0, keepdims=True) for total in totals]
    both += [sums2[2:3, :], sums2[0:1, :], sums2[1:2, :]]
    vparts[0] = jnp.zeros(vparts.shape[1:], F32)
    vparts[1] = jnp.zeros(vparts.shape[1:], F32)
    for number, line in enumerate(both):
        for side in range(split):
            at = number * split + side
            part = line[:, side * inner : (side + 1) * inner]
            vparts[0, at : at + 1, :] = part
            vparts[1, at : at + 1, :] = part
    for core in range(2):
        line = jnp.sum(ups[core], axis=0, keepdims=True)
        for side in range(units // inner):
            at = 6 * split + side
            vparts[1 - core, at : at + 1, :] = line[:, side * inner : (side + 1) * inner]
    poll()

    def attend_phase(
        qkvw, tokens, tokens_t, kt, dheads_t, dheads, dk, dv, gq_t, gq, gk, gv, expo, spread
    ):
        columns = 256
        l_qkvw = [load(qkvw_h, qkvw.at[0]), load(qkvw_o, qkvw.at[1])]
        l_tokens = load(tokens_h, tokens)
        l_expo = load(expo_h.at[:, :, pl.ds(0, columns)], expo)

        for copy in crossed[3:5]:
            copy().wait_send()
        at = 2 * third
        for core in (1, 0):
            tile = dot(heads_t[core * inner : (core + 1) * inner, :], gmid16[...])
            if core == 0:
                crossed[5]().wait_recv()
            for side in range(split):
                part = tile[:, side * inner : (side + 1) * inner]
                if core == 1:
                    give(side * inner, part)
                else:
                    take(at + side * inner, part)
            if core == 1:
                cross(at, split * inner, 0)
            else:
                begin_piece(at, split * inner, "z")
        poll()
        per = heads // 2
        size = inner // per
        for core in range(2):
            tile = dot(outw[core], gmid16[...], NT)
            for head in range(per):
                rows = slice(core * inner + head * size, core * inner + (head + 1) * size)
                part = tile[head * size : (head + 1) * size] * recip[core * per + head, 0:1, :]
                dheads_t[rows, :] = part.astype(BF16)
        dheads[...] = jnp.transpose(dheads_t[...])
        kt[...] = jnp.transpose(k[...])
        poll()

        span = length[lax.axis_index("tensor")]
        lane = lax.broadcasted_iota(jnp.int32, (seq, LANES), 1)
        first = lane < size
        labels = lax.broadcasted_iota(jnp.int32, (LANES, columns), 0).astype(BF16)
        tab = jnp.zeros((32, LANES), F32)
        for part in range(seq // columns):
            start = part * columns
            here = slice(start, start + columns)
            l_expo.wait()

            def pair_back(pair, carry, here=here, part=part):
                cols = pl.ds(pl.multiple_of(pair * LANES, LANES), LANES)
                values, queries = v[:, cols], q[here, cols]
                grads, grads_t = dheads[here, cols], dheads_t[cols, here]
                gvs, gks = [], []
                for side in range(2):
                    head = 2 * pair + side
                    mine = first if side == 0 else jnp.logical_not(first)
                    back = dot(jnp.where(mine, values, jnp.zeros_like(values)), grads_t)
                    chance = expo[head].astype(F32)
                    product = chance * back
                    shift = jnp.sum(product, axis=0, keepdims=True) * recip[head, 0:1, here]
                    gscore = product - chance * shift
                    for half in range(columns // LANES):
                        spread[pl.ds(half * seq * 16 + head, seq, stride=16), :] = gscore[
                            :, half * LANES : (half + 1) * LANES
                        ]
                    gscore = gscore.astype(BF16)
                    gvs.append(dot(expo[head], grads))
                    gks.append(dot(gscore, queries))
                    rows = pl.ds(pl.multiple_of(pair * LANES + side * size, size), size)
                    gq_t[rows, here] = (dot(kt[rows, :], gscore) * 0.125).astype(BF16)
                gvalue = jnp.where(first, gvs[0], gvs[1])
                gkey = jnp.where(first, gks[0], gks[1])
                if part == 0:
                    dv[:, cols] = gvalue
                    dk[:, cols] = gkey
                else:
                    gv[:, cols] = (dv[:, cols] + gvalue).astype(BF16)
                    gk[:, cols] = (dk[:, cols] + gkey).astype(BF16)
                return carry

            for group in range(heads // 4):
                lax.fori_loop(2 * group, 2 * group + 2, pair_back, 0)
                poll()
            if part + 1 < seq // columns:
                l_expo = load(expo_h.at[:, :, pl.ds(start + columns, columns)], expo)

            position = lax.broadcasted_iota(jnp.int32, (1, columns), 1) + start
            inside = (position < span).astype(F32)

            def count(number, carry, here=here, inside=inside):
                rows = pl.ds(pl.multiple_of(number * 16, 16), 16)
                index = bucket[rows, here]
                grads = jnp.concatenate(
                    [
                        spread[pl.ds(pl.multiple_of(half * seq * 16 + number * 256, 256), 256), :]
                        for half in range(columns // LANES)
                    ],
                    axis=1,
                )
                for line in range(16):
                    hot = jnp.where(
                        labels == index[line : line + 1, :],
                        jnp.ones((), BF16),
                        jnp.zeros((), BF16),
                    )
                    other = jnp.where(number * 16 + line < span, 1.0 - inside, inside)
                    some = grads[16 * line : 16 * line + 16]
                    far = some * other
                    both = jnp.concatenate([some - far, far], axis=0).astype(BF16)
                    carry = carry + dot(both, hot, NT)
                return carry

            tab = lax.fori_loop(0, seq // 16, count, tab)
            poll()

        gq[...] = jnp.transpose(gq_t[...])
        l_tokens.wait()
        tokens_t[...] = jnp.transpose(tokens[...])
        at = 2 * third + split * inner
        kinds = (gq, gk, gv)
        for core in (1, 0):
            for kind in range(3):
                if core == 0:
                    crossed[6 + kind]().wait_recv()
                for top in range(0, width, 256):
                    tile = dot(
                        tokens_t[top : top + 256, :],
                        kinds[kind][:, core * inner : (core + 1) * inner],
                    )
                    if core == 1:
                        give(split * inner + kind * width + top, tile)
                    else:
                        take(at + kind * width + top, tile)
                if core == 1:
                    cross(at + kind * width, width, split * inner + kind * width)
                else:
                    begin_piece(at + kind * width, width, "xyz"[kind])
                poll()

        for core in range(2):
            mine = slice(core * inner, (core + 1) * inner)
            at = 6 * split + units // inner
            for number, kind in ((0, gq), (1, gv)):
                line = jnp.sum(fold8(kind[:, mine].astype(F32)), axis=0, keepdims=True)
                vparts[1 - core, at + number : at + number + 1, :] = line
            for half in range(2):
                rows = slice(half * 16 + core * per, half * 16 + (core + 1) * per)
                cols = slice(half * LANES, (half + 1) * LANES)
                vparts[1 - core, 24 : 24 + per, cols] = tab[rows]
        Vectors(vparts, vland, small, bits, kit, vs_sem, vr_sem).run(0)
        poll()

        l_qkvw[0].wait()
        l_qkvw[1].wait()

        def token_tile(number, carry):
            cols = pl.ds(pl.multiple_of(number * 256, 256), 256)
            total = wide[:, cols]
            for core in range(2):
                for kind in range(3):
                    total = total + dot(
                        kinds[kind][:, core * inner : (core + 1) * inner],
                        qkvw[core, kind, cols, :],
                        NT,
                    )
            wide[:, cols] = total
            return carry

        lax.fori_loop(0, width // 256, token_tile, 0)

    pl.run_scoped(
        attend_phase,
        pltpu.VMEM((2,) + qkvw_h.shape, BF16),
        pltpu.VMEM((seq, width), BF16),
        pltpu.VMEM((width, seq), BF16),
        pltpu.VMEM((2 * inner, seq), BF16),
        pltpu.VMEM((2 * inner, seq), BF16),
        pltpu.VMEM((seq, 2 * inner), BF16),
        pltpu.VMEM((seq, 2 * inner), F32),
        pltpu.VMEM((seq, 2 * inner), F32),
        pltpu.VMEM((2 * inner, seq), BF16),
        pltpu.VMEM((seq, 2 * inner), BF16),
        pltpu.VMEM((seq, 2 * inner), BF16),
        pltpu.VMEM((seq, 2 * inner), BF16),
        pltpu.VMEM((heads, seq, 256), BF16),
        pltpu.VMEM((2 * seq * 16, LANES), F32),
    )
    done = pltpu.make_async_copy(wide, gtok_h, out_sem.at[0])
    done.start()
    last = polls[0]
    for number in range(last, max(plan) + 1):
        for piece, step in plan.get(number, ()):
            kit.pieces[piece].run(step)
    done.wait()
    for piece in kit.pieces:
        piece.finish()
    for copy in crossed[5:]:
        copy().wait_send()


def backward(plan, bits, saved, weights, others, tokens, sums2, gain1, bucket, length):
    seq, width = tokens.shape
    qkvw, outw, upw, downw = weights
    inner = qkvw.shape[2]
    units = upw.shape[1]
    heads = saved[-1].shape[0]
    shape = jax.ShapeDtypeStruct
    here = pl.BlockSpec(memory_space=pltpu.VMEM)
    away = pl.BlockSpec(memory_space=pl.ANY)
    scalar = pl.BlockSpec(memory_space=pltpu.SMEM)
    rows = (3 * width * inner + inner * width + 2 * width * units) // inner
    levels = min(4, bits)
    lands = rows - (rows >> levels) + (bits - levels) * (rows >> levels)
    slots = 9 * (2 * levels + bits - levels)
    return pl.pallas_call(
        functools.partial(backward_kernel, plan, bits),
        out_shape=(
            shape((rows, inner), BF16),
            shape((seq, width), F32),
            shape((32, inner), F32),
        ),
        in_specs=[away] * 22 + [here] * 3 + [scalar],
        out_specs=(away, away, here),
        scratch_shapes=[
            pltpu.VMEM((rows, inner), BF16),
            pltpu.VMEM((rows // 3, inner), BF16),
            pltpu.VMEM((rows, inner), BF16),
            pltpu.VMEM((lands, inner), BF16),
            pltpu.VMEM((seq, width), BF16),
            pltpu.VMEM((seq, width), F32),
            pltpu.VMEM((seq, width), F32),
            pltpu.VMEM((seq, LANES), F32),
            pltpu.VMEM((2 * inner, seq), BF16),
            pltpu.VMEM((2, inner, width), BF16),
            pltpu.VMEM((seq, width), BF16),
            pltpu.VMEM((seq, width), F32),
            pltpu.VMEM((seq, 2 * inner), BF16),
            pltpu.VMEM((seq, 2 * inner), BF16),
            pltpu.VMEM((seq, 2 * inner), BF16),
            pltpu.VMEM((heads, 8, seq), F32),
            pltpu.VMEM((2, 8, units), F32),
            pltpu.VMEM((bits + 1, 32, inner), F32),
            pltpu.VMEM((bits + 1, 32, inner), F32),
            pltpu.SemaphoreType.DMA((32,)),
            pltpu.SemaphoreType.DMA((1,)),
            pltpu.SemaphoreType.DMA((slots,)),
            pltpu.SemaphoreType.DMA((slots,)),
            pltpu.SemaphoreType.DMA((9,)),
            pltpu.SemaphoreType.DMA((9,)),
            pltpu.SemaphoreType.DMA((9,)),
            pltpu.SemaphoreType.DMA((bits + 1,)),
            pltpu.SemaphoreType.DMA((bits + 1,)),
        ],
        compiler_params=pltpu.CompilerParams(
            collective_id=1, has_side_effects=True, vmem_limit_bytes=VMEM_LIMIT
        ),
    )(*saved, qkvw, outw, upw, downw, *others, tokens, sums2, gain1, bucket, length)


def order_of_steps(levels, bits):
    late = []
    for step in range(1, 2 * levels + 1):
        late += [(number, step) for number in range(9)]
        if step <= bits + 1:
            late.append((9, step))
    for step in range(2 * levels + 1, bits + 2):
        late.append((9, step))
    return {64: tuple(late)}


def on_device(
    dp,
    tokens,
    qkv_weight,
    qv_bias,
    rel_table,
    out_weight,
    out_bias,
    norm1_gain,
    norm1_bias,
    up_weight,
    up_bias,
    down_weight,
    down_bias,
    norm2_gain,
    norm2_bias,
    rel_bucket,
    query_len,
    key_mask,
    upstream,
):
    width = tokens.shape[1]
    inner = qkv_weight.shape[2]
    units = up_weight.shape[1]
    qkvw = jnp.transpose(qkv_weight, (1, 0, 2))
    bucket = rel_bucket.T
    saved = forward(
        tokens,
        qkvw,
        qv_bias,
        rel_table.T,
        out_weight,
        out_bias,
        norm1_gain,
        norm1_bias,
        up_weight,
        up_bias.reshape(1, units),
        down_weight,
        down_bias,
        norm2_gain,
        norm2_bias,
        bucket,
        query_len,
        key_mask,
        upstream,
    )
    (
        out,
        gsec,
        gbr,
        act,
        slope,
        first,
        normed1,
        inverse1,
        heads_t,
        q,
        k,
        v,
        expo,
        recip,
        qkvw_o,
        outw_o,
        upw_o,
        downw_o,
        sums2,
    ) = saved
    bits = int(math.log2(dp))
    flat, grad_tokens, small = backward(
        order_of_steps(min(4, bits), bits),
        bits,
        (gbr, act, slope, first, gsec, normed1, inverse1, heads_t, q, k, v, expo, recip),
        (qkvw, out_weight, up_weight, down_weight),
        (qkvw_o, outw_o, upw_o, downw_o),
        tokens,
        sums2,
        norm1_gain,
        bucket.astype(BF16),
        query_len,
    )
    split = width // inner
    third = flat.shape[0] // 3
    down = flat[:third].reshape(units // 256, split, 256, inner)
    grad_down = jnp.transpose(down, (0, 2, 1, 3)).reshape(units, width).astype(F32)
    up = flat[third : 2 * third].reshape(units // inner, width, inner)
    grad_up = jnp.transpose(up, (1, 0, 2)).reshape(width, units).astype(F32)
    grad_out = flat[2 * third : 2 * third + split * inner].reshape(split, inner, inner)
    grad_out = jnp.transpose(grad_out, (1, 0, 2)).reshape(inner, width).astype(F32)
    grad_mix = flat[2 * third + split * inner :].reshape(3, width, inner)
    grad_mix = jnp.transpose(grad_mix, (1, 0, 2)).astype(F32)

    def vector(number):
        return small[number * split : (number + 1) * split].reshape(width)

    at = 6 * split
    heads = rel_table.shape[1]
    return (
        out,
        grad_tokens,
        grad_mix,
        small[at + units // inner : at + units // inner + 2],
        small[24 : 24 + heads, : 2 * LANES].T,
        grad_out,
        vector(0),
        vector(1),
        vector(2),
        grad_up,
        small[at : at + units // inner].reshape(units),
        grad_down,
        vector(3),
        vector(4),
        vector(5),
    )


def solution(mesh):
    rows = P(("dp", "tensor"), None)
    whole = P()
    in_specs = (
        rows,
        P(None, None, "tensor"),
        P(None, "tensor"),
        P(None, "tensor"),
        P("tensor", None),
        whole,
        whole,
        whole,
        P(None, "tensor"),
        P("tensor"),
        P("tensor", None),
        whole,
        whole,
        whole,
        whole,
        P("dp"),
        P("dp", None),
        rows,
    )
    out_specs = (
        rows,
        rows,
        P(None, None, "tensor"),
        P(None, "tensor"),
        P(None, "tensor"),
        P("tensor", None),
        whole,
        whole,
        whole,
        P(None, "tensor"),
        P("tensor"),
        P("tensor", None),
        whole,
        whole,
        whole,
    )
    return jax.shard_map(
        functools.partial(on_device, mesh.shape["dp"]),
        mesh=mesh,
        in_specs=in_specs,
        out_specs=out_specs,
        check_vma=False,
    )
```

time: 981 us -> 262 us (0.27); the launches traced: 970 us -> 261 us
  matrix products: 379 us -> 0 us
  Pallas kernels: 0 us -> 229 us
  waiting for transfers between devices: 198 us -> 0 us
  local copies, waits for them, and re-layouts: 158 us -> 27.9 us
  blocking collectives: 122 us -> 0 us
  other arithmetic: 84.7 us -> 3.88 us
  between operations: 14.7 us -> 0.74 us
  loops' own time: 13 us -> 0 us
    dot_general x49 -> x0, matrix products: 379 us -> none  [the longest x8 105 us: fold_bucket_rows(): jnp.einsum('ijb,chij->cbh', onehot, grads, precision=lax.Precision.HIGHEST)]
    pallas_call x0 -> x2, Pallas kernels: none -> 229 us  [the longest x1 195 us: backward(): pl.pallas_call(functools.partial(backward_kernel, plan, bits), out_shape=...]
    psum x1 -> x0, waiting for transfers between devices: 134 us -> none  [on_device(): lax.psum((grad_weight_mixed, grad_qv, grad_table, grad_out, grad_up, grad...]
    psum x2 -> x0, blocking collectives: 122 us -> none  [the longest x1 77.5 us: on_device(): lax.psum((grad_weight_mixed, grad_qv, grad_table, grad_out, grad_up, grad...]
    while x62 -> x0, local copies, waits for them, and re-layouts: 59.4 us -> none  [the longest x7 28.4 us: forward(): lax.map(partial(pair_forward, terms), (query.reshape(shape), keys.reshape...]
    all_gather x6 -> x0, waiting for transfers between devices: 32.4 us -> none  [the longest x2 21.6 us: forward(): lax.all_gather(first.astype(jnp.bfloat16), 'tensor', axis=0, tiled=True)]
    reduce_scatter x6 -> x0, waiting for transfers between devices: 30.7 us -> none  [the longest x2 13.7 us: forward(): lax.psum_scatter(jnp.dot(heads_out, weight_out, preferred_element_type=jn...]
    another operation x8 -> x0, other arithmetic: 25.5 us -> none  [the longest x4 25.4 us: pair_backward(): jnp.stack([jnp.where(crossing[None], zeros, grad_scores), jnp.where(cross...]
  transfers between devices with their start and end apart: 13 -> 0, of which waited for: 7 -> 0; matrix products, arithmetic and copies ran while one was open for 40% -> 0% of each run, Pallas kernels for 0% -> 0%
where the time goes in v1:
time: 262 us; the launch traced here: 261 us
  Pallas kernels  229 us (87%)
  local copies, waits for them, and re-layouts  27.9 us (11%)
  other arithmetic  3.88 us (1%)
    pallas_call x1, Pallas kernels, backward(): pl.pallas_call(functools.partial(backward_kernel, plan, bits), out_shape=...  195 us
    pallas_call x1, Pallas kernels, forward(): pl.pallas_call(forward_kernel, out_shape=out_shape, in_specs=[away] * 9 +...  34.2 us
    unnamed x12, local copies, waits for them, and re-layouts  7.34 us

profile of v1, /device:TPU:0, one launch (start us, length us, event | category | flops | bytes accessed | tf_op | source)
XLA Modules:
  0.0 261.3 jit_solution(15368725426562780491)
XLA Ops:
  0.6 1.3 reshape.75.upb_h
  1.9 1.6 copy.33
  3.5 0.0 copy-start
  3.5 1.0 bitcast_convert_fusion.bucket
  4.6 0.1 copy-done
  4.6 34.2 %shard_map.289 = (bf16[512,768]{1,0:T(8,128)(2,1)}, f32[512,768]{1,0:T(8,128)}, bf16[512,768]{1,0:T(8,128)(2,1)}, bf16[512,3072]{1,0:T(8,128)(2,1)}, bf16[512,30...) custom-call(bf16[512,768]{1,0:T(8,128)(2,1)} %tokens_h.3, ...), custom_call_target="tpu_custom_call" | custom-call | tf_op jit(solution)/shard_map/pallas_call | solution.py:447
  38.9 194.6 %shard_map.290 = (bf16[9216,384]{1,0:T(8,128)(2,1)}, f32[512,768]{1,0:T(8,128)}, f32[32,384]{1,0:T(8,128)}) custom-call(bf16[512,768]{1,0:T(8,128)(2,1)} %get-tuple-element.38.gbr_h, bf16[512,3072]{1,0:T(8,128)(2,1)} %get-tuple-element.39.act_h, bf16[512,3072]{1,0:T(8,128)(2,1)} %get-tuple-element.40.slope_h, bf16[512,768]{1,0:T(8,128)(2,1)} %get-tuple-element.41.first_h, ...), custom_call_target="tpu_custom_call" | custom-call | tf_op jit(solution)/shard_map/pallas_call | solution.py:1162
  233.5 0.7 slice.47
  234.2 0.6 reshape.79
  234.8 1.3 slice_bitcast_fusion
  236.1 1.4 fusion.1
  237.5 0.6 reshape.82
  238.1 0.6 reshape.81
  238.7 0.6 reshape.80
  239.3 0.6 reshape.78
  239.9 0.6 reshape.77
  240.5 0.6 reshape.76
  241.1 1.1 slice.42
  242.3 0.0 copy-start.1
  242.3 0.1 convert_bitcast_fusion.3
  242.4 1.1 copy.37
  243.5 2.4 slice.39
  245.9 0.4 copy-done.1
  246.2 0.5 fusion
  246.7 2.0 convert_bitcast_fusion.2
  248.7 0.3 convert_bitcast_fusion.1
  249.0 2.8 %copy.38 = f32[4,96,8,384]{3,2,0,1:T(8,128)} copy(f32[4,96,8,384]{3,2,1,0:T(8,128)S(1)} %convert_bitcast_fusion.1) | data formatting | bytes 9437184 | tf_op jit(solution)/shard_map/convert_element_type | solution.py:1303
  251.9 0.4 convert_bitcast_fusion
  252.3 3.6 %copy.36 = f32[6,256,2,384]{3,2,1,0:T(2,128)S(1)} copy(f32[6,256,2,384]{3,1,2,0:T(8,128)S(1)} %convert_bitcast_fusion) | data formatting | bytes 9437184 | tf_op jit(solution)/shard_map/convert_element_type | solution.py:1301
  256.0 0.0 copy-start.3
  256.0 2.5 copy.39
  258.5 0.0 copy-start.2
  258.5 0.0 copy-done.3
  258.5 0.9 copy.42
  259.4 0.8 copy-done.2
  260.2 1.1 copy.43
Async XLA Ops:
  3.5 1.1 copy-start
  242.3 4.0 %copy-start.1 = (bf16[9216,384]{1,0:T(8,128)(2,1)S(1)}, bf16[9216,384]{1,0:T(8,128)(2,1)}, u32[]{:S(2)}) copy-start(bf16[9216,384]{1,0:T(8,128)(2,1)} %get-tuple-element.57) | copy-start | bytes 21233668
  256.0 2.5 copy-start.3
  258.5 1.7 copy-start.2

commit v2 on v1

--- a/solution.py
+++ b/solution.py
@@ -17,6 +17,53 @@
 NT = (((1,), (1,)), ((), ()))
 TN = (((0,), (0,)), ((), ()))
 VMEM_LIMIT = 62 * 2**20
+ORDERS = {
+    "down": ((1, "xyzZ"), (2, "yxzZ"), (3, "zZyx")),
+    "up": ((1, "xyzZ"), (1, "yxzZ"), (1, "xyzZ"), (1, "yxzZ")),
+    "out": "xyzZ",
+    "mix": ("xyzZ", "yzZx", "xyzZ"),
+}
+PAUSES = {
+    5: ((0, 1),),
+    12: ((1, 1),),
+    13: ((0, 2),),
+    17: ((2, 1), (0, 3)),
+    18: ((3, 1), (4, 1)),
+    19: ((1, 2),),
+    20: ((6, 1),),
+    21: ((3, 2), (5, 1)),
+    22: ((2, 2), (4, 2)),
+    23: ((0, 4), (1, 3)),
+    24: ((5, 2), (3, 3)),
+    25: ((4, 3), (7, 1), (2, 3), (0, 5)),
+    26: ((1, 4), (5, 3), (6, 2)),
+    27: ((3, 4), (2, 4), (7, 2), (4, 4), (0, 6)),
+    28: ((1, 5),),
+    29: ((2, 5), (5, 4), (6, 3), (0, 7), (3, 5)),
+    30: ((7, 3), (4, 5)),
+    31: ((1, 6), (2, 6), (5, 5)),
+    32: ((0, 8), (6, 4), (3, 6)),
+    33: ((7, 4), (4, 6)),
+    34: ((1, 7),),
+    35: ((3, 7),),
+    36: ((4, 7),),
+    37: ((5, 6),),
+    40: ((2, 7), (3, 8), (1, 8)),
+    41: ((6, 5), (7, 5)),
+    47: ((4, 8),),
+    48: ((5, 7),),
+    49: ((8, 1),),
+    50: ((2, 8),),
+    51: ((9, 1), (6, 6), (7, 6)),
+    52: ((10, 1), (8, 2)),
+    53: ((9, 2), (7, 7)),
+    54: ((8, 3), (5, 8)),
+    55: ((10, 2),),
+    56: ((9, 3), (6, 7)),
+    57: ((8, 4),),
+    58: ((10, 3),),
+}
+TAIL = ((8, 5), (7, 8), (10, 4), (9, 4), (6, 8), (8, 6), (9, 5), (10, 5), (8, 7), (9, 6), (10, 6), (9, 7), (10, 7), (8, 8), (9, 8), (10, 8))
 
 
 def dot(left, right, dims=None):
@@ -127,6 +174,7 @@
     outw_o,
     upw_o,
     downw_o,
+    bucket_o,
     sums,
     tokens,
     qkvw,
@@ -135,8 +183,11 @@
     outw,
     upw,
     upb,
+    upb_other,
+    upb_rows,
     downw,
     upstream,
+    bucket_t,
     packed,
     valid,
     q,
@@ -177,7 +228,7 @@
             (tab_h, tab.at[0]),
             (outw_h, outw.at[0]),
             (upw_h, upw.at[0]),
-            (upb_h, upb.at[0]),
+            (upb_h, upb),
             (downw_h, downw.at[0]),
             (upstream_h, upstream),
         )
@@ -195,7 +246,7 @@
             (tab_h, tab.at[1]),
             (outw_h, outw.at[1]),
             (upw_h, upw.at[1]),
-            (upb_h, upb.at[1]),
+            (upb_h, upb_other),
             (downw_h, downw.at[1]),
         )
     ):
@@ -221,6 +272,8 @@
     span = length[me]
     mine = mask[pl.ds(me, 1), :].astype(F32)
     valid[...] = jnp.transpose(jnp.broadcast_to(mine, (LANES, seq)))
+    bucket_t[...] = jnp.transpose(bucket[...])
+    bucket_o[...] = bucket_t[...].astype(BF16)
 
     def mix(core):
         rows = tokens[...]
@@ -248,7 +301,7 @@
     store(qkvw.at[1], qkvw_o)
 
     def attend(pair, carry):
-        attend_pair(pair, q, k, vt, packed, bucket, valid, span, step, expo, heads_t, recip)
+        attend_pair(pair, q, k, vt, packed, bucket_t, valid, span, step, expo, heads_t, recip)
         return carry
 
     lax.fori_loop(0, 2 * pairs, attend, 0)
@@ -293,15 +346,17 @@
         if core == 0:
             loads[5].wait()
             loads[6].wait()
+            upb_rows[0] = row(upb)
         else:
             sends[4].wait_recv()
             sends[5].wait_recv()
+            upb_rows[1] = row(upb_other)
             store(upw.at[1], upw_o)
 
         def expand(tile, carry, core=core):
             cols = pl.ds(pl.multiple_of(tile * 256, 256), 256)
             here = pl.ds(pl.multiple_of(core * half_units + tile * 256, 256), 256)
-            hidden = dot(first16[...], upw[core, :, cols]) + upb[core, :, cols]
+            hidden = dot(first16[...], upw[core, :, cols]) + upb_rows[core, :, cols]
             chance = 0.5 * (1.0 + lax.erf(hidden * math.sqrt(0.5)))
             density = jnp.exp(hidden * hidden * -0.5) * (1.0 / math.sqrt(2.0 * math.pi))
             act[:, here] = (hidden * chance).astype(BF16)
@@ -408,6 +463,7 @@
         shape(outw.shape, BF16),
         shape(upw.shape, BF16),
         shape(downw.shape, BF16),
+        shape((seq, seq), BF16),
         shape((8, width), F32),
     )
     scratch = [
@@ -417,9 +473,12 @@
         pltpu.VMEM((2,) + tab.shape, F32),
         pltpu.VMEM((2,) + outw.shape, BF16),
         pltpu.VMEM((2,) + upw.shape, BF16),
-        pltpu.VMEM((2,) + upb.shape, F32),
+        pltpu.VMEM(upb.shape, F32),
+        pltpu.VMEM(upb.shape, F32),
+        pltpu.VMEM((2, 1, units), F32),
         pltpu.VMEM((2,) + downw.shape, BF16),
         pltpu.VMEM((seq, width), BF16),
+        pltpu.VMEM((seq, seq), jnp.int32),
         pltpu.VMEM((heads // 2, 8, 2 * LANES), jnp.int32),
         pltpu.VMEM((seq, LANES), F32),
         pltpu.VMEM((seq, 2 * inner), BF16),
@@ -448,7 +507,7 @@
         forward_kernel,
         out_shape=out_shape,
         in_specs=[away] * 9 + [here] * 7 + [scalar, here],
-        out_specs=(away,) * 18 + (here,),
+        out_specs=(away,) * 18 + (here, here),
         scratch_shapes=scratch,
         compiler_params=pltpu.CompilerParams(
             collective_id=0, has_side_effects=True, vmem_limit_bytes=VMEM_LIMIT
@@ -527,7 +586,6 @@
         ]
         self.crossing = [(kit.slot(), kit.room(length >> len(order))) for _ in extra]
         self.spreading = [kit.slot() for _ in order]
-        self.sent = []
 
     def begin(self, levels):
         at = self.start
@@ -597,7 +655,6 @@
             self.add(self.begin(step), self.halving[step - 1][1], self.length >> step)
         if step < levels:
             self.halve(step).start()
-            self.sent.append(functools.partial(self.halve, step))
             return
         if step == levels:
             for number in range(len(self.extra)):
@@ -612,11 +669,11 @@
                 self.keep().wait()
         if step < 2 * levels:
             self.spread(step - levels).start()
-            self.sent.append(functools.partial(self.spread, step - levels))
 
     def finish(self):
-        for sent in self.sent:
-            sent().wait_send()
+        for level in range(len(self.bits)):
+            self.halve(level).wait_send()
+            self.spread(level).wait_send()
 
 
 class Vectors:
@@ -718,7 +775,7 @@
     inner = outw.shape[1]
     units = upw_h.shape[1]
     heads = recip.shape[0]
-    levels = min(4, bits)
+    levels = 4
 
     barrier = pltpu.get_barrier_semaphore()
     pl.semaphore_signal(barrier, inc=1, device_id=other_core(), device_id_type=MESH)
@@ -734,11 +791,6 @@
         return copy
 
     kit = Kit(acc, landing, result_h, send_sem, recv_sem, local_sem)
-    orders = {
-        "x": tuple(range(levels)),
-        "y": ((1, 0) + tuple(range(2, levels)))[:levels] if levels > 1 else tuple(range(levels)),
-        "z": tuple(range(2, levels)) + tuple(range(min(2, levels))),
-    }
     extra = tuple(range(levels, bits))
     crossed = []
 
@@ -760,13 +812,34 @@
 
     polls = [0]
 
+    def run_steps(number):
+        for piece, step in plan.get(number, ()):
+            kit.pieces[piece].run(step)
+
     def poll():
-        for number, step in plan.get(polls[0], ()):
-            kit.pieces[number].run(step)
+        run_steps(polls[0])
         polls[0] += 1
 
+    def polled_loop(low, high, body, initial, every=1):
+        start = polls[0]
+        pauses = (high - low) // every
+        polls[0] += pauses
+        busy = [number for number in range(pauses) if plan.get(start + number)]
+
+        def turn(index, carry):
+            carry = body(index, carry)
+            for number in busy:
+
+                @pl.when(index == low + (number + 1) * every - 1)
+                def _():
+                    run_steps(start + number)
+
+            return carry
+
+        return lax.fori_loop(low, high, turn, initial)
+
     def begin_piece(start, size, order):
-        fresh = Piece(start, size, orders[order], extra, kit)
+        fresh = Piece(start, size, tuple("xyzZ".index(axis) for axis in order), extra, kit)
         fresh.run(0)
 
     def give(place, tile):
@@ -806,12 +879,12 @@
         pl.semaphore_wait(barrier, 1 + bits)
 
         tiles = units // 256
-        group = tiles // 3
         span = 256 * split
         l_gbr.wait()
         for core in (1, 0):
             l_act[core].wait()
-            for part in range(3):
+            low = 0
+            for part, (count, order) in enumerate(ORDERS["down"]):
                 if core == 0:
                     crossed[part]().wait_recv()
 
@@ -825,40 +898,39 @@
                         )
                     return carry
 
-                lax.fori_loop(part * group, (part + 1) * group, down_tile, 0)
-                start = part * group * span
+                lax.fori_loop(low, low + count, down_tile, 0)
                 if core == 1:
-                    cross(start, group * span, start)
+                    cross(low * span, count * span, low * span)
                 else:
-                    begin_piece(start, group * span, "xyz"[part])
+                    begin_piece(low * span, count * span, order)
                     poll()
+                low += count
+        fed = len(crossed)
 
         l_slope.wait()
         for core in (1, 0):
             l_down[core].wait()
-            for part in range(2):
-
-                def slope_tile(number, carry, core=core):
-                    here = pl.ds(pl.multiple_of(number * 256, 256), 256)
-                    cols = pl.ds(pl.multiple_of(core * units + number * 256, 256), 256)
-                    tile = dot(gbr[...], downw[core, here, :], NT) * slope[:, cols].astype(F32)
-                    tile = tile.astype(BF16)
-                    slope[:, cols] = tile
-                    ups[core, :, here] = fold8(tile.astype(F32))
-                    return carry
-
-                lax.fori_loop(part * (tiles // 2), (part + 1) * (tiles // 2), slope_tile, 0)
-                poll()
+
+            def slope_tile(number, carry, core=core):
+                here = pl.ds(pl.multiple_of(number * 256, 256), 256)
+                cols = pl.ds(pl.multiple_of(core * units + number * 256, 256), 256)
+                tile = dot(gbr[...], downw[core, here, :], NT) * slope[:, cols].astype(F32)
+                tile = tile.astype(BF16)
+                slope[:, cols] = tile
+                ups[core, :, here] = fold8(tile.astype(F32))
+                return carry
+
+            polled_loop(0, tiles, slope_tile, 0, tiles // 2)
 
         l_first.wait()
         first_t[...] = jnp.transpose(first[...])
-        for copy in crossed[:3]:
+        for copy in crossed[:fed]:
             copy().wait_send()
-        blocks = units // inner
         for core in (1, 0):
-            for part in range(2):
+            low = 0
+            for part, (count, order) in enumerate(ORDERS["up"]):
                 if core == 0:
-                    crossed[3 + part]().wait_recv()
+                    crossed[fed + part]().wait_recv()
 
                 def up_tile(number, carry, core=core):
                     cols = pl.ds(pl.multiple_of(core * units + number * inner, LANES), inner)
@@ -870,14 +942,13 @@
                             take(third + number * width + top, tile)
                     return carry
 
-                lax.fori_loop(part * (blocks // 2), (part + 1) * (blocks // 2), up_tile, 0)
-                size = (blocks // 2) * width
+                lax.fori_loop(low, low + count, up_tile, 0)
                 if core == 1:
-                    cross(third + part * size, size, part * size)
+                    cross(third + low * width, count * width, low * width)
                 else:
-                    begin_piece(third + part * size, size, "xy"[part])
+                    begin_piece(third + low * width, count * width, order)
                 poll()
-
+                low += count
         l_up[0].wait()
         l_up[1].wait()
         l_late[0].wait()
@@ -891,8 +962,7 @@
             )
             return carry
 
-        lax.fori_loop(0, width // 256, first_tile, 0)
-        poll()
+        polled_loop(0, width // 256, first_tile, 0)
         for copy in l_late[1:]:
             copy.wait()
 
@@ -933,16 +1003,12 @@
     vparts[0] = jnp.zeros(vparts.shape[1:], F32)
     vparts[1] = jnp.zeros(vparts.shape[1:], F32)
     for number, line in enumerate(both):
-        for side in range(split):
-            at = number * split + side
-            part = line[:, side * inner : (side + 1) * inner]
-            vparts[0, at : at + 1, :] = part
-            vparts[1, at : at + 1, :] = part
+        vparts[0, number : number + 1, :] = line
+        vparts[1, number : number + 1, :] = line
     for core in range(2):
         line = jnp.sum(ups[core], axis=0, keepdims=True)
-        for side in range(units // inner):
-            at = 6 * split + side
-            vparts[1 - core, at : at + 1, :] = line[:, side * inner : (side + 1) * inner]
+        for side in range(units // width):
+            vparts[1 - core, 6 + side : 7 + side, :] = line[:, side * width : (side + 1) * width]
     poll()
 
     def attend_phase(
@@ -953,13 +1019,14 @@
         l_tokens = load(tokens_h, tokens)
         l_expo = load(expo_h.at[:, :, pl.ds(0, columns)], expo)
 
-        for copy in crossed[3:5]:
+        full = len(crossed)
+        for copy in crossed[full - len(ORDERS["up"]) :]:
             copy().wait_send()
         at = 2 * third
         for core in (1, 0):
             tile = dot(heads_t[core * inner : (core + 1) * inner, :], gmid16[...])
             if core == 0:
-                crossed[5]().wait_recv()
+                crossed[full]().wait_recv()
             for side in range(split):
                 part = tile[:, side * inner : (side + 1) * inner]
                 if core == 1:
@@ -969,7 +1036,7 @@
             if core == 1:
                 cross(at, split * inner, 0)
             else:
-                begin_piece(at, split * inner, "z")
+                begin_piece(at, split * inner, ORDERS["out"])
         poll()
         per = heads // 2
         size = inner // per
@@ -1025,9 +1092,7 @@
                     gk[:, cols] = (dk[:, cols] + gkey).astype(BF16)
                 return carry
 
-            for group in range(heads // 4):
-                lax.fori_loop(2 * group, 2 * group + 2, pair_back, 0)
-                poll()
+            polled_loop(0, heads // 2, pair_back, 0)
             if part + 1 < seq // columns:
                 l_expo = load(expo_h.at[:, :, pl.ds(start + columns, columns)], expo)
 
@@ -1057,8 +1122,8 @@
                     carry = carry + dot(both, hot, NT)
                 return carry
 
-            tab = lax.fori_loop(0, seq // 16, count, tab)
-            poll()
+            if part + 1 < seq // columns:
+                tab = polled_loop(0, seq // 16, count, tab, 4)
 
         gq[...] = jnp.transpose(gq_t[...])
         l_tokens.wait()
@@ -1068,7 +1133,7 @@
         for core in (1, 0):
             for kind in range(3):
                 if core == 0:
-                    crossed[6 + kind]().wait_recv()
+                    crossed[full + 1 + kind]().wait_recv()
                 for top in range(0, width, 256):
                     tile = dot(
                         tokens_t[top : top + 256, :],
@@ -1081,19 +1146,20 @@
                 if core == 1:
                     cross(at + kind * width, width, split * inner + kind * width)
                 else:
-                    begin_piece(at + kind * width, width, "xyz"[kind])
+                    begin_piece(at + kind * width, width, ORDERS["mix"][kind])
                 poll()
+
+        tab = polled_loop(0, seq // 16, count, tab, 4)
 
         for core in range(2):
             mine = slice(core * inner, (core + 1) * inner)
-            at = 6 * split + units // inner
             for number, kind in ((0, gq), (1, gv)):
                 line = jnp.sum(fold8(kind[:, mine].astype(F32)), axis=0, keepdims=True)
-                vparts[1 - core, at + number : at + number + 1, :] = line
+                vparts[1 - core, 8:9, number * inner : (number + 1) * inner] = line
             for half in range(2):
                 rows = slice(half * 16 + core * per, half * 16 + (core + 1) * per)
                 cols = slice(half * LANES, (half + 1) * LANES)
-                vparts[1 - core, 24 : 24 + per, cols] = tab[rows]
+                vparts[1 - core, 10 : 10 + per, cols] = tab[rows]
         Vectors(vparts, vland, small, bits, kit, vs_sem, vr_sem).run(0)
         poll()
 
@@ -1113,7 +1179,7 @@
             wide[:, cols] = total
             return carry
 
-        lax.fori_loop(0, width // 256, token_tile, 0)
+        polled_loop(0, width // 256, token_tile, 0)
 
     pl.run_scoped(
         attend_phase,
@@ -1134,14 +1200,11 @@
     )
     done = pltpu.make_async_copy(wide, gtok_h, out_sem.at[0])
     done.start()
-    last = polls[0]
-    for number in range(last, max(plan) + 1):
-        for piece, step in plan.get(number, ()):
-            kit.pieces[piece].run(step)
+    run_steps("tail")
     done.wait()
     for piece in kit.pieces:
         piece.finish()
-    for copy in crossed[5:]:
+    for copy in crossed[-4:]:
         copy().wait_send()
 
 
@@ -1156,15 +1219,16 @@
     away = pl.BlockSpec(memory_space=pl.ANY)
     scalar = pl.BlockSpec(memory_space=pltpu.SMEM)
     rows = (3 * width * inner + inner * width + 2 * width * units) // inner
-    levels = min(4, bits)
+    levels = 4
     lands = rows - (rows >> levels) + (bits - levels) * (rows >> levels)
-    slots = 9 * (2 * levels + bits - levels)
+    pieces = len(ORDERS["down"]) + len(ORDERS["up"]) + 4
+    slots = pieces * (2 * levels + bits - levels)
     return pl.pallas_call(
         functools.partial(backward_kernel, plan, bits),
         out_shape=(
             shape((rows, inner), BF16),
             shape((seq, width), F32),
-            shape((32, inner), F32),
+            shape((16, width), F32),
         ),
         in_specs=[away] * 22 + [here] * 3 + [scalar],
         out_specs=(away, away, here),
@@ -1186,15 +1250,15 @@
             pltpu.VMEM((seq, 2 * inner), BF16),
             pltpu.VMEM((heads, 8, seq), F32),
             pltpu.VMEM((2, 8, units), F32),
-            pltpu.VMEM((bits + 1, 32, inner), F32),
-            pltpu.VMEM((bits + 1, 32, inner), F32),
+            pltpu.VMEM((bits + 1, 16, width), F32),
+            pltpu.VMEM((bits + 1, 16, width), F32),
             pltpu.SemaphoreType.DMA((32,)),
             pltpu.SemaphoreType.DMA((1,)),
             pltpu.SemaphoreType.DMA((slots,)),
             pltpu.SemaphoreType.DMA((slots,)),
-            pltpu.SemaphoreType.DMA((9,)),
-            pltpu.SemaphoreType.DMA((9,)),
-            pltpu.SemaphoreType.DMA((9,)),
+            pltpu.SemaphoreType.DMA((pieces,)),
+            pltpu.SemaphoreType.DMA((pieces,)),
+            pltpu.SemaphoreType.DMA((pieces,)),
             pltpu.SemaphoreType.DMA((bits + 1,)),
             pltpu.SemaphoreType.DMA((bits + 1,)),
         ],
@@ -1204,15 +1268,164 @@
     )(*saved, qkvw, outw, upw, downw, *others, tokens, sums2, gain1, bucket, length)
 
 
-def order_of_steps(levels, bits):
-    late = []
-    for step in range(1, 2 * levels + 1):
-        late += [(number, step) for number in range(9)]
-        if step <= bits + 1:
-            late.append((9, step))
-    for step in range(2 * levels + 1, bits + 2):
-        late.append((9, step))
-    return {64: tuple(late)}
+def finish_kernel(
+    flat_h,
+    out_h,
+    gtok_h,
+    small,
+    out_f,
+    gtok_f,
+    mix_f,
+    gqv,
+    gtab,
+    gout_f,
+    goutb,
+    gain1,
+    shift1,
+    up_f,
+    gupb,
+    down_f,
+    gdownb,
+    gain2,
+    shift2,
+    flat,
+    mix,
+    gout,
+    up,
+    down,
+    gtok,
+    out,
+    in_sem,
+    out_sem,
+):
+    rows, inner = flat.shape
+    units, width = down.shape
+    split = width // inner
+    third = rows // 3
+    copies = []
+    tiles = units // 256
+    span = 256 * split
+    sizes = (
+        [span] * tiles + [width] * (units // inner) + [split * inner] + [width] * 3
+    )
+    loads = []
+    at = 0
+    for number, size in enumerate(sizes):
+        here = pl.ds(at, size)
+        loads.append(pltpu.make_async_copy(flat_h.at[here, :], flat.at[here, :], in_sem.at[number]))
+        loads[-1].start()
+        at += size
+
+    for source, target in ((gtok_h, gtok), (out_h, out)):
+        loads.append(pltpu.make_async_copy(source, target, in_sem.at[len(loads)]))
+        loads[-1].start()
+
+    def store(source, target):
+        copies.append(pltpu.make_async_copy(source, target, out_sem.at[len(copies)]))
+        copies[-1].start()
+
+    def wide(start, size):
+        return flat[start : start + size, :].astype(F32)
+
+    for tile in range(tiles):
+        loads[tile].wait()
+        here = slice(tile * 256, tile * 256 + 256)
+        for side in range(split):
+            down[here, side * inner : (side + 1) * inner] = wide(tile * span + side * 256, 256)
+        here = pl.ds(tile * 256, 256)
+        store(down.at[here, :], down_f.at[here, :])
+    for part in range(units // inner):
+        loads[tiles + part].wait()
+        cols = pl.ds(part * inner, inner)
+        up[:, cols] = wide(third + part * width, width)
+        store(up.at[:, cols], up_f.at[:, cols])
+    at = 2 * third
+    loads[-6].wait()
+    for side in range(split):
+        gout[:, side * inner : (side + 1) * inner] = wide(at + side * inner, inner)
+    store(gout, gout_f)
+    at += split * inner
+    for kind in range(3):
+        loads[kind - 5].wait()
+        mix[kind] = wide(at + kind * width, width)
+        store(mix.at[kind], mix_f.at[kind])
+    loads[-2].wait()
+    store(gtok, gtok_f)
+    loads[-1].wait()
+    store(out, out_f)
+    for number, vector in enumerate((goutb, gain1, shift1, gdownb, gain2, shift2)):
+        vector[...] = small[number : number + 1, :].reshape(width)
+    gupb[...] = jnp.concatenate(
+        [small[6 + side : 7 + side, :] for side in range(units // width)], axis=1
+    ).reshape(units)
+    for kind in range(2):
+        gqv[kind : kind + 1, :] = small[8:9, kind * inner : (kind + 1) * inner]
+    gtab[...] = small[10 : 10 + gtab.shape[0], : gtab.shape[1]]
+    for copy in copies:
+        copy.wait()
+
+
+def finish(flat, small, out, grad_tokens, width, units, heads):
+    shape = jax.ShapeDtypeStruct
+    here = pl.BlockSpec(memory_space=pltpu.VMEM)
+    away = pl.BlockSpec(memory_space=pl.ANY)
+    inner = flat.shape[1]
+    vector = shape((width,), F32)
+    got = pl.pallas_call(
+        finish_kernel,
+        out_shape=(
+            shape(out.shape, BF16),
+            shape(grad_tokens.shape, F32),
+            shape((3, width, inner), F32),
+            shape((2, inner), F32),
+            shape((heads, 2 * LANES), F32),
+            shape((inner, width), F32),
+            vector,
+            vector,
+            vector,
+            shape((width, units), F32),
+            shape((units,), F32),
+            shape((units, width), F32),
+            vector,
+            vector,
+            vector,
+        ),
+        in_specs=[away] * 3 + [here],
+        out_specs=(away, away, away, here, here, away, here, here, here, away, here, away)
+        + (here,) * 3,
+        scratch_shapes=[
+            pltpu.VMEM(flat.shape, BF16),
+            pltpu.VMEM((3, width, inner), F32),
+            pltpu.VMEM((inner, width), F32),
+            pltpu.VMEM((width, units), F32),
+            pltpu.VMEM((units, width), F32),
+            pltpu.VMEM(grad_tokens.shape, F32),
+            pltpu.VMEM(out.shape, BF16),
+            pltpu.SemaphoreType.DMA((units // 256 + units // inner + 6,)),
+            pltpu.SemaphoreType.DMA((units // 256 + units // inner + 6,)),
+        ],
+        compiler_params=pltpu.CompilerParams(vmem_limit_bytes=VMEM_LIMIT),
+    )(flat, out, grad_tokens, small)
+    got = list(got)
+    got[2] = jnp.transpose(got[2], (1, 0, 2))
+    got[4] = got[4].T
+    return tuple(got)
+
+
+def order_of_steps(bits):
+    pieces = len(ORDERS["down"]) + len(ORDERS["up"]) + 4
+    plan = dict(PAUSES)
+    done = {(piece, step) for steps in PAUSES.values() for piece, step in steps}
+    rest = [(piece, step) for piece, step in TAIL if (piece, step) not in done]
+    small = [(pieces, step) for step in range(1, bits + 2)]
+    every = max(1, len(rest) // (len(small) + 1))
+    tail = []
+    for number, step in enumerate(rest):
+        tail.append(step)
+        if number % every == every - 1 and small:
+            tail.append(small.pop(0))
+    plan["tail"] = tuple(tail + small)
+    return plan
 
 
 def on_device(
@@ -1240,7 +1453,6 @@
     inner = qkv_weight.shape[2]
     units = up_weight.shape[1]
     qkvw = jnp.transpose(qkv_weight, (1, 0, 2))
-    bucket = rel_bucket.T
     saved = forward(
         tokens,
         qkvw,
@@ -1251,12 +1463,12 @@
         norm1_gain,
         norm1_bias,
         up_weight,
-        up_bias.reshape(1, units),
+        up_bias,
         down_weight,
         down_bias,
         norm2_gain,
         norm2_bias,
-        bucket,
+        rel_bucket,
         query_len,
         key_mask,
         upstream,
@@ -1280,11 +1492,12 @@
         outw_o,
         upw_o,
         downw_o,
+        bucket,
         sums2,
     ) = saved
     bits = int(math.log2(dp))
     flat, grad_tokens, small = backward(
-        order_of_steps(min(4, bits), bits),
+        order_of_steps(bits),
         bits,
         (gbr, act, slope, first, gsec, normed1, inverse1, heads_t, q, k, v, expo, recip),
         (qkvw, out_weight, up_weight, down_weight),
@@ -1292,42 +1505,10 @@
         tokens,
         sums2,
         norm1_gain,
-        bucket.astype(BF16),
+        bucket,
         query_len,
     )
-    split = width // inner
-    third = flat.shape[0] // 3
-    down = flat[:third].reshape(units // 256, split, 256, inner)
-    grad_down = jnp.transpose(down, (0, 2, 1, 3)).reshape(units, width).astype(F32)
-    up = flat[third : 2 * third].reshape(units // inner, width, inner)
-    grad_up = jnp.transpose(up, (1, 0, 2)).reshape(width, units).astype(F32)
-    grad_out = flat[2 * third : 2 * third + split * inner].reshape(split, inner, inner)
-    grad_out = jnp.transpose(grad_out, (1, 0, 2)).reshape(inner, width).astype(F32)
-    grad_mix = flat[2 * third + split * inner :].reshape(3, width, inner)
-    grad_mix = jnp.transpose(grad_mix, (1, 0, 2)).astype(F32)
-
-    def vector(number):
-        return small[number * split : (number + 1) * split].reshape(width)
-
-    at = 6 * split
-    heads = rel_table.shape[1]
-    return (
-        out,
-        grad_tokens,
-        grad_mix,
-        small[at + units // inner : at + units // inner + 2],
-        small[24 : 24 + heads, : 2 * LANES].T,
-        grad_out,
-        vector(0),
-        vector(1),
-        vector(2),
-        grad_up,
-        small[at : at + units // inner].reshape(units),
-        grad_down,
-        vector(3),
-        vector(4),
-        vector(5),
-    )
+    return finish(flat, small, out, grad_tokens, width, units, rel_table.shape[1])
 
 
 def solution(mesh):

time: 262 us -> 193 us (0.74)
  Pallas kernels: 229 us -> 192 us
  local copies, waits for them, and re-layouts: 27.9 us -> 0 us
  other arithmetic: 3.88 us -> 0 us
    pallas_call x1, Pallas kernels: 195 us -> 147 us  [backward(): pl.pallas_call(functools.partial(backward_kernel, plan, bits), out_shape=...]
    pallas_call x0 -> x1, Pallas kernels: none -> 10.4 us  [finish(): pl.pallas_call(finish_kernel, out_shape=(shape(out.shape, BF16), shape(gr...]
    convert_element_type x3 -> x0, local copies, waits for them, and re-layouts: 7.59 us -> none  [the longest x1 3.64 us: on_device(): jnp.transpose(down, (0, 2, 1, 3)).reshape(units, width).astype(F32)]
    unnamed x12 -> x0, local copies, waits for them, and re-layouts: 7.34 us -> none
    slice x5 -> x0, local copies, waits for them, and re-layouts: 6.15 us -> none  [the longest x1 2.4 us: on_device(): grad_mix = flat[2 * third + split * inner:].reshape(3, width, inner)]
    reshape x8 -> x0, local copies, waits for them, and re-layouts: 5.5 us -> none  [the longest x6 3.6 us: vector(): return small[number * split:(number + 1) * split].reshape(width)]
    convert_element_type x3 -> x0, other arithmetic: 3.5 us -> none  [the longest x1 2.02 us: on_device(): grad_mix = jnp.transpose(grad_mix, (1, 0, 2)).astype(F32)]
where the time goes in v2:
time: 193 us
  Pallas kernels  192 us (99%)
    pallas_call x1, Pallas kernels, backward(): pl.pallas_call(functools.partial(backward_kernel, plan, bits), out_shape=...  147 us
    pallas_call x1, Pallas kernels, forward(): pl.pallas_call(forward_kernel, out_shape=out_shape, in_specs=[away] * 9 +...  34.5 us
    pallas_call x1, Pallas kernels, finish(): pl.pallas_call(finish_kernel, out_shape=(shape(out.shape, BF16), shape(gr...  10.4 us

profile of v2, /device:TPU:0, one launch (start us, length us, event | category | flops | bytes accessed | tf_op | source)
XLA Modules:
  0.0 192.8 jit_solution(10882050161571062901)
XLA Ops:
  0.6 34.5 %shard_map.289 = (bf16[512,768]{1,0:T(8,128)(2,1)}, f32[512,768]{1,0:T(8,128)}, bf16[512,768]{1,0:T(8,128)(2,1)}, bf16[512,3072]{1,0:T(8,128)(2,1)}, bf16[512,30...) custom-call(bf16[512,768]{1,0:T(8,128)(2,1)} %tokens_h.3, ...), custom_call_target="tpu_custom_call" | custom-call | tf_op jit(solution)/shard_map/pallas_call | solution.py:506
  35.2 147.0 %shard_map.290 = (bf16[9216,384]{1,0:T(8,128)(2,1)}, f32[512,768]{1,0:T(8,128)}, f32[16,768]{1,0:T(8,128)}) custom-call(bf16[512,768]{1,0:T(8,128)(2,1)} %get-tuple-element.53.gbr_h, bf16[512,3072]{1,0:T(8,128)(2,1)} %get-tuple-element.54.act_h, bf16[512,3072]{1,0:T(8,128)(2,1)} %get-tuple-element.55.slope_h, bf16[512,768]{1,0:T(8,128)(2,1)} %get-tuple-element.56.first_h, ...), custom_call_target="tpu_custom_call" | custom-call | tf_op jit(solution)/shard_map/pallas_call | solution.py:1226
  182.3 10.4 %shard_map.291 = (bf16[512,768]{1,0:T(8,128)(2,1)}, f32[512,768]{1,0:T(8,128)}, f32[3,768,384]{2,1,0:T(8,128)}, f32[2,384]{1,0:T(2,128)}, f32[6,256]{1,0:T(8,128...) custom-call(bf16[9216,384]{1,0:T(8,128)(2,1)} %get-tuple-element.72., ...), custom_call_target="tpu_custom_call" | custom-call | tf_op jit(solution)/shard_map/pallas_call | solution.py:1374

commit v3 on v2

v3 whole, which is shorter than its diff:
```python
import functools
import math

import jax
import jax.numpy as jnp
from jax import lax
from jax.experimental import pallas as pl
from jax.experimental.pallas import tpu as pltpu
from jax.sharding import PartitionSpec as P

EPSILON = 1e-05
FAR_BELOW = -1000000000.0
MESH = pl.DeviceIdType.MESH
F32 = jnp.float32
BF16 = jnp.bfloat16
LANES = 128
NT = (((1,), (1,)), ((), ()))
TN = (((0,), (0,)), ((), ()))
VMEM_LIMIT = 62 * 2**20
ORDERS = {
    "down": ((2, "zZyx", "xyzZ"), (4, "yxzZ", "zZxy")),
    "up": ((2, "xyD", "yxD"), (2, "xyD", "yxD")),
    "out": ("zZyx", "xyzZ"),
    "mix": (("xyD", "yxD"), ("xyD", "xyD"), ("xyD", "yxD")),
}
PAUSES = {
    8: ((0, 1),),
    14: ((1, 1),),
    15: ((2, 1), (0, 2)),
    18: ((4, 1), (3, 1)),
    19: ((1, 2), (0, 3)),
    20: ((2, 2), (4, 2)),
    21: ((3, 2),),
    22: ((1, 3), (0, 4)),
    27: ((4, 3),),
    28: ((2, 3),),
    32: ((5, 1),),
    33: ((3, 3),),
    34: ((1, 4),),
    35: ((0, 5),),
    36: ((6, 1),),
    38: ((7, 1), (4, 4)),
    40: ((5, 2),),
    41: ((2, 4), (6, 2)),
    42: ((7, 2),),
    45: ((3, 4),),
    46: ((8, 1), (2, 5), (0, 6), (1, 5), (4, 5)),
}
TAIL = ((5, 3), (3, 5), (8, 2), (6, 3), (7, 3), (2, 6), (1, 6), (0, 7), (4, 6), (5, 4), (3, 6), (8, 3), (6, 4), (7, 4), (6, 5), (5, 5), (7, 5), (0, 8), (1, 7), (8, 4), (4, 7), (6, 6), (5, 6), (7, 6), (8, 5), (1, 8), (4, 8))


def dot(left, right, dims=None):
    if dims is None:
        return jnp.dot(left, right, preferred_element_type=F32)
    return lax.dot_general(left, right, dims, preferred_element_type=F32)


def other_core():
    return {"tensor": 1 - lax.axis_index("tensor")}


def row(ref):
    return ref[...].reshape(1, ref.shape[-1])


def fold8(block):
    return jnp.sum(block.reshape(block.shape[0] // 8, 8, block.shape[1]), axis=0)


def pack_tables(tab, packed):
    step = jnp.maximum(jnp.max(jnp.abs(tab[...])), 1e-30) / 32000.0
    inverse = 1.0 / step
    heads = tab.shape[1]
    for core in range(2):
        for pair in range(heads // 2):
            high = tab[core, 2 * pair : 2 * pair + 1, :] * inverse
            low = jnp.round(tab[core, 2 * pair + 1 : 2 * pair + 2, :] * inverse)
            high = jnp.round(high - low * (1 / 65536.0))
            both = high.astype(jnp.int32) * 65536 + low.astype(jnp.int32)
            packed[core * (heads // 2) + pair] = jnp.broadcast_to(both, packed.shape[1:])
    return step


def attend_pair(pair, q, k, vt, packed, bucket, valid, length, step, expo, heads_t, recip):
    seq = q.shape[0]
    cols = pl.ds(pl.multiple_of(pair * LANES, LANES), LANES)
    keys = k[:, cols]
    queries = q[:, cols]
    lane = lax.broadcasted_iota(jnp.int32, (seq, LANES), 1)
    in_query = lax.broadcasted_iota(jnp.int32, (seq, LANES), 0) < length
    terms = packed[pair, 0:1, :]
    near = jnp.broadcast_to(terms[:, :LANES], (seq, LANES))
    far = jnp.broadcast_to(terms[:, LANES:], (seq, LANES))
    same = jnp.where(in_query, far, near)
    swap = jnp.where(in_query, near, far)
    pieces = ([], [])
    for start in range(0, seq, LANES):
        index = bucket[:, start : start + LANES]
        got = jnp.take_along_axis(same, index, axis=1, mode="promise_in_bounds")
        if start == 0:
            turned = jnp.take_along_axis(swap, index, axis=1, mode="promise_in_bounds")
            got = jnp.where(lane < length, turned, got)
        pieces[0].append(got.astype(F32) * (step * (1 / 65536.0)))
        pieces[1].append(jnp.left_shift(got, 16).astype(F32) * (step * (1 / 65536.0)))
    first = lane < LANES // 2
    real = jnp.concatenate([valid[...] > 0] * (seq // LANES), axis=1)
    for side in range(2):
        mine = first if side == 0 else jnp.logical_not(first)
        scores = dot(jnp.where(mine, keys, jnp.zeros_like(keys)), queries, NT)
        scores = scores + jnp.concatenate(pieces[side], axis=1)
        scores = jnp.where(real, scores, FAR_BELOW)
        highest = jnp.max(scores, axis=0, keepdims=True)
        weights = jnp.exp(scores - highest).astype(BF16)
        expo[2 * pair + side] = weights
        rows = pl.ds(pl.multiple_of(pair * LANES + side * 64, 64), 64)
        values = jnp.concatenate([vt[rows, :], jnp.ones((16, seq), BF16)], axis=0)
        got = dot(values, weights)
        inverse = 1.0 / got[64:65]
        heads_t[rows, :] = (got[:64] * inverse).astype(BF16)
        recip[2 * pair + side] = jnp.broadcast_to(inverse, recip.shape[1:])


def dp_stride(bits):
    first, second = 1 << bits[0], 1 << bits[1]
    if first == second:
        return first
    return first + lax.axis_index("tensor") * (second - first)


def dp_side(bits):
    return lax.rem(lax.div(lax.axis_index("dp"), dp_stride(bits)), 2)


def dp_partner(bits):
    return {"dp": lax.axis_index("dp") + (1 - 2 * dp_side(bits)) * dp_stride(bits)}


def dp_quarter(ahead):
    return lax.rem(lax.div(lax.axis_index("dp"), 4) + ahead, 4)


def dp_ahead(ahead):
    return {"dp": lax.axis_index("dp") + 4 * (dp_quarter(ahead) - dp_quarter(0))}


def flat_rows(start, size):
    return pl.ds(pl.multiple_of(start, 16), size)


class Kit:
    def __init__(self, acc, landing, result, send_sem, recv_sem, local_sem):
        self.acc, self.landing, self.result = acc, landing, result
        self.send_sem, self.recv_sem, self.local_sem = send_sem, recv_sem, local_sem
        self.used = 0
        self.landed = 0
        self.pieces = []

    def slot(self):
        self.used += 1
        return self.used - 1

    def room(self, size):
        self.landed += size
        return self.landed - size

    def remote(self, slot, source, target, device):
        return pltpu.make_async_remote_copy(
            src_ref=source,
            dst_ref=target,
            send_sem=self.send_sem.at[slot],
            recv_sem=self.recv_sem.at[slot],
            device_id=device,
            device_id_type=MESH,
        )


class Piece:
    def __init__(self, start, length, stages, extra, kit):
        self.start = start
        self.stages, self.extra = stages, extra
        self.kit = kit
        self.number = len(kit.pieces)
        self.steps = 2 * len(stages) + 1
        kit.pieces.append(self)
        self.sizes = [length]
        self.cutting, self.spreading = [], []
        for stage in stages:
            parts = 4 if stage is None else 2
            size = self.sizes[-1] // parts
            self.sizes.append(size)
            self.cutting.append([(kit.slot(), kit.room(size)) for _ in range(parts - 1)])
            self.spreading.append([kit.slot() for _ in range(parts - 1)])
        self.crossing = [(kit.slot(), kit.room(self.sizes[-1])) for _ in extra]

    def begin(self, levels):
        at = self.start
        for level in range(levels):
            stage = self.stages[level]
            at = at + (dp_quarter(0) if stage is None else dp_side(stage)) * self.sizes[level + 1]
        return at

    def partners(self, stage):
        if stage is None:
            return [(dp_quarter(ahead), dp_ahead(ahead)) for ahead in (1, 2, 3)]
        return [(1 - dp_side(stage), dp_partner(stage))]

    def cut(self, level):
        kit, size = self.kit, self.sizes[level + 1]
        at = self.begin(level)
        return [
            kit.remote(
                slot,
                kit.acc.at[flat_rows(at + part * size, size), :],
                kit.landing.at[pl.ds(room, size), :],
                device,
            )
            for (slot, room), (part, device) in zip(
                self.cutting[level], self.partners(self.stages[level])
            )
        ]

    def swap(self, number):
        kit = self.kit
        slot, room = self.crossing[number]
        size = self.sizes[-1]
        return kit.remote(
            slot,
            kit.acc.at[flat_rows(self.begin(len(self.stages)), size), :],
            kit.landing.at[pl.ds(room, size), :],
            dp_partner(self.extra[number]),
        )

    def keep(self):
        kit = self.kit
        mine = flat_rows(self.begin(len(self.stages)), self.sizes[-1])
        return pltpu.make_async_copy(
            kit.acc.at[mine, :], kit.result.at[mine, :], kit.local_sem.at[self.number]
        )

    def spread(self, level):
        kit = self.kit
        mine = flat_rows(self.begin(level + 1), self.sizes[level + 1])
        source = kit.acc if level == len(self.stages) - 1 else kit.result
        return [
            kit.remote(slot, source.at[mine, :], kit.result.at[mine, :], device)
            for slot, (_, device) in zip(
                self.spreading[level], self.partners(self.stages[level])
            )
        ]

    def add(self, target, rooms, size):
        kit = self.kit
        chunk = math.gcd(size, 192)

        def some(number, carry):
            there = flat_rows(target + number * chunk, chunk)
            total = kit.acc[there, :].astype(F32)
            for room in rooms:
                total = total + kit.landing[flat_rows(room + number * chunk, chunk), :].astype(F32)
            kit.acc[there, :] = total.astype(BF16)
            return carry

        lax.fori_loop(0, size // chunk, some, 0)

    def run(self, step):
        levels = len(self.stages)
        if 0 < step <= levels:
            for copy in self.cut(step - 1):
                copy.wait_recv()
            rooms = [room for _, room in self.cutting[step - 1]]
            self.add(self.begin(step), rooms, self.sizes[step])
        if step < levels:
            for copy in self.cut(step):
                copy.start()
            return
        if step == levels:
            for number in range(len(self.extra)):
                both = self.swap(number)
                both.start()
                both.wait()
                self.add(self.begin(levels), [self.crossing[number][1]], self.sizes[-1])
            self.keep().start()
        else:
            for copy in self.spread(2 * levels - step):
                copy.wait_recv()
            if step == levels + 1:
                self.keep().wait()
        if step < 2 * levels:
            for copy in self.spread(2 * levels - 1 - step):
                copy.start()

    def finish(self):
        for level in range(len(self.stages)):
            for copy in self.cut(level) + self.spread(level):
                copy.wait_send()


class Vectors:
    def __init__(self, parts, landing, result, bits, kit, send_sem, recv_sem):
        self.parts, self.landing, self.result = parts, landing, result
        self.bits = bits
        self.steps = bits + 2
        self.send_sem, self.recv_sem = send_sem, recv_sem
        kit.pieces.append(self)

    def exchange(self, step):
        return pltpu.make_async_remote_copy(
            src_ref=self.parts.at[step],
            dst_ref=self.landing.at[step],
            send_sem=self.send_sem.at[step],
            recv_sem=self.recv_sem.at[step],
            device_id=other_core() if step == 0 else dp_partner((step - 1, step - 1)),
            device_id_type=MESH,
        )

    def run(self, step):
        if step > 0:
            self.exchange(step - 1).wait_recv()
            total = self.parts[max(step - 1, 1)] + self.landing[step - 1]
            if step <= self.bits:
                self.parts[step] = total
            else:
                self.result[...] = total
        if step <= self.bits:
            self.exchange(step).start()

    def finish(self):
        for step in range(self.bits + 1):
            self.exchange(step).wait_send()


def layer_kernel(
    plan,
    bits,
    tokens_h,
    qkvw_h,
    qvb_h,
    tab_h,
    outw_h,
    upw_h,
    upb_h,
    downw_h,
    upstream_h,
    bucket_h,
    outb,
    gain1,
    shift1,
    downb,
    gain2,
    shift2,
    mask,
    length,
    result_h,
    gtok_h,
    out_h,
    small,
    qkvw_o,
    outw_o,
    upw_o,
    downw_o,
    expo_h,
    acc,
    xsend,
    xrecv,
    landing,
    tokens,
    qvb,
    tab,
    upb,
    upb_other,
    upb_rows,
    outw,
    q,
    k,
    v,
    heads_t,
    recip,
    bucket,
    wide,
    gmid16,
    upstream,
    ups,
    vparts,
    vland,
    in_sem,
    out_sem,
    send_sem,
    recv_sem,
    local_sem,
    xs_sem,
    xr_sem,
    vs_sem,
    vr_sem,
    ws_sem,
    wr_sem,
):
    seq, width = tokens.shape
    inner = outw.shape[1]
    units = upw_h.shape[1]
    heads = recip.shape[0]
    pairs = inner // LANES
    split = width // inner
    third = acc.shape[0] // 3

    barrier = pltpu.get_barrier_semaphore()
    pl.semaphore_signal(barrier, inc=1, device_id=other_core(), device_id_type=MESH)
    for bit in range(bits):
        pl.semaphore_signal(barrier, inc=1, device_id=dp_partner((bit, bit)), device_id_type=MESH)
    pl.semaphore_signal(
        barrier,
        inc=1,
        device_id={"dp": lax.axis_index("dp") + 12 - 8 * dp_quarter(0)},
        device_id_type=MESH,
    )

    used, stored = [], []

    def load(source, target):
        copy = pltpu.make_async_copy(source, target, in_sem.at[len(used)])
        used.append(copy)
        copy.start()
        return copy

    loaded = []

    def early(source, target):
        number = len(used)
        used.append(None)
        loaded.append(lambda: pltpu.make_async_copy(source, target(), in_sem.at[number]))
        loaded[-1]().start()

    def store(source, target):
        copy = pltpu.make_async_copy(source, target, out_sem.at[len(stored)])
        stored.append(copy)
        copy.start()
        return copy

    halves = [
        (qkvw_h, qkvw_o),
        (qvb_h, qvb.at[1]),
        (tab_h, tab.at[1]),
        (outw_h, outw_o),
        (upw_h, upw_o),
        (upb_h, upb_other),
        (downw_h, downw_o),
    ]

    def half(number):
        source, target = halves[number]
        return pltpu.make_async_remote_copy(
            src_ref=source,
            dst_ref=target,
            send_sem=ws_sem.at[number],
            recv_sem=wr_sem.at[number],
            device_id=other_core(),
            device_id_type=MESH,
        )

    kit = Kit(acc, landing, result_h, send_sem, recv_sem, local_sem)
    extra = tuple((bit, bit) for bit in range(4, bits))
    crossed = []

    def cross(start, size, place):
        number = len(crossed)

        def copy():
            return pltpu.make_async_remote_copy(
                src_ref=xsend.at[pl.ds(place, size), :],
                dst_ref=xrecv.at[pl.ds(start, size), :],
                send_sem=xs_sem.at[number],
                recv_sem=xr_sem.at[number],
                device_id=other_core(),
                device_id_type=MESH,
            )

        copy().start()
        crossed.append(copy)

    polls = [0]

    def run_steps(number):
        for piece, step in plan.get(number, ()):
            kit.pieces[piece].run(step)

    def poll():
        run_steps(polls[0])
        polls[0] += 1

    def polled_loop(low, high, body, initial, every=1):
        start = polls[0]
        pauses = (high - low) // every
        polls[0] += pauses
        busy = [number for number in range(pauses) if plan.get(start + number)]

        def turn(index, carry):
            carry = body(index, carry)
            for number in busy:

                @pl.when(index == low + (number + 1) * every - 1)
                def _():
                    run_steps(start + number)

            return carry

        return lax.fori_loop(low, high, turn, initial)

    def begin_piece(start, size, orders):
        order = tuple(
            None if one == "D" else ("xyzZ".index(one), "xyzZ".index(two))
            for one, two in zip(*orders)
        )
        fresh = Piece(start, size, order, extra, kit)
        fresh.run(0)

    def give(place, tile):
        xsend[flat_rows(place, tile.shape[0]), :] = tile.astype(BF16)

    def take(start, tile):
        there = flat_rows(start, tile.shape[0])
        acc[there, :] = (tile + xrecv[there, :].astype(F32)).astype(BF16)

    me = lax.axis_index("tensor")

    def attend_phase(upw, downw, qkvw, vt, bucket_i, bucket_t, valid, packed, expo):
        l_tokens = load(tokens_h, tokens)
        l_qkvw = load(qkvw_h, qkvw.at[0])
        l_qvb = load(qvb_h, qvb.at[0])
        l_bucket = load(bucket_h, bucket_i)
        l_tab = load(tab_h, tab.at[0])
        l_late = [load(outw_h, outw.at[0]), load(upb_h, upb)]
        early(upw_h, lambda: upw.at[0])
        early(downw_h, lambda: downw.at[0])
        early(upstream_h, lambda: upstream)
        pl.semaphore_wait(barrier, 2 + bits)
        for number in range(3):
            half(number).start()
        span = length[me]
        mine = mask[pl.ds(me, 1), :].astype(F32)
        valid[...] = jnp.transpose(jnp.broadcast_to(mine, (LANES, seq)))

        def mix(core):
            rows = tokens[...]
            cols = slice(core * inner, (core + 1) * inner)
            query = dot(rows, qkvw[core, 0])
            q[:, cols] = ((query + qvb[core, 0:1, :]) * 0.125).astype(BF16)
            k[:, cols] = dot(rows, qkvw[core, 1]).astype(BF16)
            value = (dot(rows, qkvw[core, 2]) + qvb[core, 1:2, :]).astype(BF16)
            v[:, cols] = value
            vt[cols, :] = jnp.transpose(value)

        l_tokens.wait()
        l_qkvw.wait()
        l_qvb.wait()
        mix(0)
        l_bucket.wait()
        bucket_t[...] = jnp.transpose(bucket_i[...])
        bucket[...] = bucket_t[...].astype(BF16)
        l_tab.wait()
        half(2).wait_recv()
        step = pack_tables(tab, packed)

        def attend(pair, carry):
            attend_pair(pair, q, k, vt, packed, bucket_t, valid, span, step, expo, heads_t, recip)
            return carry

        kept = []

        def keep(low, high):
            here = pl.ds(2 * low, 2 * (high - low))
            kept.append(store(expo.at[here], expo_h.at[here]))

        lax.fori_loop(0, 1, attend, 0)
        half(0).wait_recv()
        half(1).wait_recv()
        l_other = load(qkvw_o, qkvw.at[1])
        for number in range(3, 6):
            half(number).start()
        lax.fori_loop(1, pairs, attend, 0, unroll=2)
        keep(0, pairs)
        l_other.wait()
        mix(1)
        lax.fori_loop(pairs, pairs + 1, attend, 0)
        keep(pairs, pairs + 1)
        half(6).start()
        half(3).wait_recv()
        l_late.append(load(outw_o, outw.at[1]))
        lax.fori_loop(pairs + 1, 2 * pairs, attend, 0, unroll=2)
        keep(pairs + 1, 2 * pairs)
        half(4).wait_recv()
        early(upw_o, lambda: upw.at[1])
        for copy in l_late:
            copy.wait()
        lower = jnp.transpose(heads_t[...])

        def project(tile, carry):
            cols = pl.ds(pl.multiple_of(tile * 256, 256), 256)
            wide[:, cols] = dot(lower[:, :inner], outw[0, :, cols]) + dot(
                lower[:, inner:], outw[1, :, cols]
            )
            return carry

        lax.fori_loop(0, width // 256, project, 0, unroll=3)
        for copy in kept:
            copy.wait()

    def unit_phase(
        upw, downw, act, slope, first, first_t, first32, normed1, inverse1, gsec, gbr, out
    ):
        half(5).wait_recv()
        upb_rows[0] = row(upb)
        upb_rows[1] = row(upb_other)
        block = 128

        def norm_one(number, carry):
            rows = pl.ds(pl.multiple_of(number * block, block), block)
            value = wide[rows, :] + row(outb) + tokens[rows, :].astype(F32)
            center = value - jnp.mean(value, axis=-1, keepdims=True)
            inverse = lax.rsqrt(jnp.mean(center * center, axis=-1, keepdims=True) + EPSILON)
            normed = center * inverse
            result = normed * row(gain1) + row(shift1)
            normed1[rows, :] = normed
            inverse1[rows, :] = jnp.broadcast_to(inverse, (block, LANES))
            first32[rows, :] = result
            first[rows, :] = result.astype(BF16)
            return carry

        lax.fori_loop(0, seq // block, norm_one, 0, unroll=4)

        for core in range(2):
            loaded[3 * core]().wait()

            def expand(tile, carry, core=core):
                cols = pl.ds(pl.multiple_of(tile * 256, 256), 256)
                here = pl.ds(pl.multiple_of(core * units + tile * 256, 256), 256)
                hidden = dot(first[...], upw[core, :, cols]) + upb_rows[core, :, cols]
                chance = 0.5 * (1.0 + lax.erf(hidden * math.sqrt(0.5)))
                density = jnp.exp(hidden * hidden * -0.5) * (1.0 / math.sqrt(2.0 * math.pi))
                act[:, here] = (hidden * chance).astype(BF16)
                slope[:, here] = (chance + hidden * density).astype(BF16)
                return carry

            lax.fori_loop(0, units // 256, expand, 0, unroll=2)
        half(6).wait_recv()
        l_down = load(downw_o, downw.at[1])
        first_t[...] = jnp.transpose(first[...])
        loaded[1]().wait()
        l_down.wait()

        def reduce_units(tile, carry):
            cols = pl.ds(pl.multiple_of(tile * 256, 256), 256)
            wide[:, cols] = dot(act[:, :units], downw[0, :, cols]) + dot(
                act[:, units:], downw[1, :, cols]
            )
            return carry

        lax.fori_loop(0, width // 256, reduce_units, 0, unroll=3)
        loaded[2]().wait()

        def norm_two(number, carry):
            rows = pl.ds(pl.multiple_of(number * block, block), block)
            value = wide[rows, :] + row(downb) + first32[rows, :]
            center = value - jnp.mean(value, axis=-1, keepdims=True)
            inverse = lax.rsqrt(jnp.mean(center * center, axis=-1, keepdims=True) + EPSILON)
            normed = center * inverse
            out[rows, :] = (normed * row(gain2) + row(shift2)).astype(BF16)
            grad = upstream[rows, :].astype(F32)
            scaled = grad * row(gain2)
            back = inverse * (
                scaled
                - jnp.mean(scaled, axis=-1, keepdims=True)
                - normed * jnp.mean(scaled * normed, axis=-1, keepdims=True)
            )
            gsec[rows, :] = back
            gbr[rows, :] = back.astype(BF16)
            return (
                carry[0] + fold8(back),
                carry[1] + fold8(grad * normed),
                carry[2] + fold8(grad),
            )

        zero = jnp.zeros((8, width), F32)
        later = lax.fori_loop(0, seq // block, norm_two, (zero, zero, zero), unroll=4)
        kept = store(out, out_h)

        tiles = units // 256
        span = 256 * split
        for core in (1, 0):
            low = 0
            for part, (count, *order) in enumerate(ORDERS["down"]):
                if core == 0:
                    crossed[part]().wait_recv()

                def down_tile(number, carry, core=core):
                    cols = pl.ds(pl.multiple_of(core * units + number * 256, 256), 256)
                    tile = dot(act[:, cols], gbr[...], TN)
                    for side in range(split):
                        (give if core == 1 else take)(
                            number * span + side * 256,
                            tile[:, side * inner : (side + 1) * inner],
                        )
                    return carry

                lax.fori_loop(low, low + count, down_tile, 0, unroll=count)
                if core == 1:
                    cross(low * span, count * span, low * span)
                else:
                    begin_piece(low * span, count * span, order)
                    poll()
                low += count
        fed = len(crossed)

        for core in (1, 0):

            def slope_tile(number, carry, core=core):
                here = pl.ds(pl.multiple_of(number * 256, 256), 256)
                cols = pl.ds(pl.multiple_of(core * units + number * 256, 256), 256)
                tile = dot(gbr[...], downw[core, here, :], NT) * slope[:, cols].astype(F32)
                tile = tile.astype(BF16)
                slope[:, cols] = tile
                ups[core, :, here] = fold8(tile.astype(F32))
                return carry

            polled_loop(0, tiles, slope_tile, 0, tiles // 2)

        for copy in crossed[:fed]:
            copy().wait_send()
        for core in (1, 0):
            low = 0
            for part, (count, *order) in enumerate(ORDERS["up"]):
                if core == 0:
                    crossed[fed + part]().wait_recv()

                def up_tile(number, carry, core=core):
                    cols = pl.ds(pl.multiple_of(core * units + number * inner, LANES), inner)
                    for top in range(0, width, 256):
                        tile = dot(first_t[top : top + 256, :], slope[:, cols])
                        if core == 1:
                            give(number * width + top, tile)
                        else:
                            take(third + number * width + top, tile)
                    return carry

                lax.fori_loop(low, low + count, up_tile, 0)
                if core == 1:
                    cross(third + low * width, count * width, low * width)
                else:
                    begin_piece(third + low * width, count * width, order)
                poll()
                low += count

        def first_tile(number, carry):
            cols = pl.ds(pl.multiple_of(number * 256, 256), 256)
            wide[:, cols] = (
                gsec[:, cols]
                + dot(slope[:, :units], upw[0, cols, :], NT)
                + dot(slope[:, units:], upw[1, cols, :], NT)
            )
            return carry

        polled_loop(0, width // 256, first_tile, 0)
        def norm_back(number, carry):
            rows = pl.ds(pl.multiple_of(number * block, block), block)
            grad = wide[rows, :]
            normed = normed1[rows, :]
            scaled = grad * row(gain1)
            back = inverse1[rows, 0:1] * (
                scaled
                - jnp.mean(scaled, axis=-1, keepdims=True)
                - normed * jnp.mean(scaled * normed, axis=-1, keepdims=True)
            )
            wide[rows, :] = back
            gmid16[rows, :] = back.astype(BF16)
            return (
                carry[0] + fold8(back),
                carry[1] + fold8(grad * normed),
                carry[2] + fold8(grad),
            )

        totals = lax.fori_loop(0, seq // block, norm_back, (zero, zero, zero), unroll=4)
        both = [jnp.sum(total, axis=0, keepdims=True) for total in totals]
        both += [jnp.sum(total, axis=0, keepdims=True) for total in later]
        vparts[0] = jnp.zeros(vparts.shape[1:], F32)
        vparts[1] = jnp.zeros(vparts.shape[1:], F32)
        for number, line in enumerate(both):
            vparts[0, number : number + 1, :] = line
            vparts[1, number : number + 1, :] = line
        for core in range(2):
            line = jnp.sum(ups[core], axis=0, keepdims=True)
            for side in range(units // width):
                vparts[1 - core, 6 + side : 7 + side, :] = line[:, side * width : (side + 1) * width]
        poll()
        kept.wait()

    def front(upw, downw):
        pl.run_scoped(
            functools.partial(attend_phase, upw, downw),
            pltpu.VMEM((2,) + qkvw_h.shape, BF16),
            pltpu.VMEM((2 * inner, seq), BF16),
            pltpu.VMEM((seq, seq), jnp.int32),
            pltpu.VMEM((seq, seq), jnp.int32),
            pltpu.VMEM((seq, LANES), F32),
            pltpu.VMEM((heads // 2, 8, 2 * LANES), jnp.int32),
            pltpu.VMEM((heads, seq, seq), BF16),
        )
        pl.run_scoped(
            functools.partial(unit_phase, upw, downw),
            pltpu.VMEM((seq, 2 * units), BF16),
            pltpu.VMEM((seq, 2 * units), BF16),
            pltpu.VMEM((seq, width), BF16),
            pltpu.VMEM((width, seq), BF16),
            pltpu.VMEM((seq, width), F32),
            pltpu.VMEM((seq, width), F32),
            pltpu.VMEM((seq, LANES), F32),
            pltpu.VMEM((seq, width), F32),
            pltpu.VMEM((seq, width), BF16),
            pltpu.VMEM((seq, width), BF16),
        )

    pl.run_scoped(
        front,
        pltpu.VMEM((2, width, units), BF16),
        pltpu.VMEM((2, units, width), BF16),
    )

    def pair_phase(spread, gq, gk, gv, kt, dheads_t, dheads, expo, expo_sem):
        def fetch(pair):
            slot = pair % 2 if isinstance(pair, int) else lax.rem(pair, 2)
            return pltpu.make_async_copy(
                expo_h.at[pl.ds(2 * pair, 2)], expo.at[slot], expo_sem.at[slot]
            )

        fetch(0).start()

        full = len(crossed)
        for copy in crossed[full - len(ORDERS["up"]) :]:
            copy().wait_send()
        at = 2 * third
        for core in (1, 0):
            tile = dot(heads_t[core * inner : (core + 1) * inner, :], gmid16[...])
            if core == 0:
                crossed[full]().wait_recv()
            for side in range(split):
                part = tile[:, side * inner : (side + 1) * inner]
                if core == 1:
                    give(side * inner, part)
                else:
                    take(at + side * inner, part)
            if core == 1:
                cross(at, split * inner, 0)
            else:
                begin_piece(at, split * inner, ORDERS["out"])
        poll()
        for core in range(2):
            tile = dot(outw[core], gmid16[...], NT)
            for head in range(per):
                rows = slice(core * inner + head * size, core * inner + (head + 1) * size)
                part = tile[head * size : (head + 1) * size] * recip[core * per + head, 0:1, :]
                dheads_t[rows, :] = part.astype(BF16)
        dheads[...] = jnp.transpose(dheads_t[...])
        kt[...] = jnp.transpose(k[...])
        poll()
        first = lax.broadcasted_iota(jnp.int32, (seq, LANES), 1) < size

        def pair_back(pair, carry):
            cols = pl.ds(pl.multiple_of(pair * LANES, LANES), LANES)
            fetch(pair).wait()

            @pl.when(pair + 1 < heads // 2)
            def _():
                fetch(pair + 1).start()

            slot = lax.rem(pair, 2)
            values, queries = v[:, cols], q[:, cols]
            grads, grads_t = dheads[:, cols], dheads_t[cols, :]
            gvs, gks, gqs = [], [], []
            for side in range(2):
                head = 2 * pair + side
                mine = first if side == 0 else jnp.logical_not(first)
                rows = pl.ds(pl.multiple_of(pair * LANES + side * size, size), size)
                shift = jnp.sum(
                    dheads_t[rows, :].astype(F32) * heads_t[rows, :].astype(F32),
                    axis=0,
                    keepdims=True,
                )
                back = dot(jnp.where(mine, values, jnp.zeros_like(values)), grads_t)
                gscore = expo[slot, side].astype(F32) * (back - shift)
                for tile in range(seq // LANES):
                    spread[pl.ds(tile * seq * 16 + head, seq, stride=16), :] = gscore[
                        :, tile * LANES : (tile + 1) * LANES
                    ]
                gscore = gscore.astype(BF16)
                gvs.append(dot(expo[slot, side], grads))
                gks.append(dot(gscore, queries))
                gqs.append(dot(kt[rows, :], gscore) * 0.125)
            gv[:, cols] = jnp.where(first, gvs[0], gvs[1]).astype(BF16)
            gk[:, cols] = jnp.where(first, gks[0], gks[1]).astype(BF16)
            gq[:, cols] = jnp.transpose(jnp.concatenate(gqs, axis=0)).astype(BF16)
            return carry

        polled_loop(0, heads // 2, pair_back, 0)

    def mix_phase(spread, gq, gk, gv, qkvw, tokens_t):
        l_qkvw = [load(qkvw_h, qkvw.at[0]), load(qkvw_o, qkvw.at[1])]
        tokens_t[...] = jnp.transpose(tokens[...])
        full = len(crossed)
        at = 2 * third + split * inner
        kinds = (gq, gk, gv)
        for core in (1, 0):
            for kind in range(3):
                if core == 0:
                    crossed[full + kind]().wait_recv()
                for top in range(0, width, 256):
                    tile = dot(
                        tokens_t[top : top + 256, :],
                        kinds[kind][:, core * inner : (core + 1) * inner],
                    )
                    if core == 1:
                        give(split * inner + kind * width + top, tile)
                    else:
                        take(at + kind * width + top, tile)
                if core == 1:
                    cross(at + kind * width, width, split * inner + kind * width)
                else:
                    begin_piece(at + kind * width, width, ORDERS["mix"][kind])
                poll()

        span = length[me]
        columns = 256
        half_range = LANES // 2
        labels = lax.broadcasted_iota(jnp.int32, (half_range, columns), 0).astype(BF16)
        tab_sum = jnp.zeros((64, half_range), F32)
        for start in range(0, seq, columns):
            here = slice(start, start + columns)
            position = lax.broadcasted_iota(jnp.int32, (1, columns), 1) + start
            inside = (position < span).astype(F32)

            def count(number, carry, here=here, start=start, inside=inside):
                for line in range(64):
                    if line % 16 == 0:
                        at = pl.multiple_of(number * 64 + line, 16)
                        index = bucket[pl.ds(at, 16), here].astype(F32)
                        upper = (index >= half_range).astype(F32)
                        index = (index - upper * half_range).astype(BF16)
                        at = pl.multiple_of(at * 16, 256)
                        grads = jnp.concatenate(
                            [
                                spread[pl.ds(tile * seq * 16 + at, 256), :]
                                for tile in range(start // LANES, (start + columns) // LANES)
                            ],
                            axis=1,
                        )
                    turn = line % 16
                    hot = jnp.where(
                        labels == index[turn : turn + 1, :],
                        jnp.ones((), BF16),
                        jnp.zeros((), BF16),
                    )
                    other = jnp.where(number * 64 + line < span, 1.0 - inside, inside)
                    some = grads[16 * turn : 16 * turn + 16]
                    far = some * other
                    both = jnp.concatenate([some - far, far], axis=0)
                    high = both * upper[turn : turn + 1, :]
                    both = jnp.concatenate([both - high, high], axis=0).astype(BF16)
                    carry = carry + dot(both, hot, NT)
                return carry

            tab_sum = polled_loop(0, seq // 64, count, tab_sum)

        for core in range(2):
            mine = slice(core * inner, (core + 1) * inner)
            for number, kind in ((0, gq), (1, gv)):
                line = jnp.sum(fold8(kind[:, mine].astype(F32)), axis=0, keepdims=True)
                vparts[1 - core, 8:9, number * inner : (number + 1) * inner] = line
            for part in range(2):
                lines = []
                for upper in range(2):
                    at = upper * 32 + part * 16 + core * per
                    lines.append(tab_sum[at : at + per])
                cols = slice(part * LANES, (part + 1) * LANES)
                vparts[1 - core, 10 : 10 + per, cols] = jnp.concatenate(lines, axis=1)
        Vectors(vparts, vland, small, bits, kit, vs_sem, vr_sem).run(0)
        poll()

        l_qkvw[0].wait()
        l_qkvw[1].wait()

        def token_tile(number, carry):
            cols = pl.ds(pl.multiple_of(number * 256, 256), 256)
            total = wide[:, cols]
            for core in range(2):
                for kind in range(3):
                    total = total + dot(
                        kinds[kind][:, core * inner : (core + 1) * inner],
                        qkvw[core, kind, cols, :],
                        NT,
                    )
            wide[:, cols] = total
            return carry

        polled_loop(0, width // 256, token_tile, 0)

    per = heads // 2
    size = inner // per

    def back(spread, gq, gk, gv):
        pl.run_scoped(
            functools.partial(pair_phase, spread, gq, gk, gv),
            pltpu.VMEM((2 * inner, seq), BF16),
            pltpu.VMEM((2 * inner, seq), BF16),
            pltpu.VMEM((seq, 2 * inner), BF16),
            pltpu.VMEM((2, 2, seq, seq), BF16),
            pltpu.SemaphoreType.DMA((2,)),
        )
        pl.run_scoped(
            functools.partial(mix_phase, spread, gq, gk, gv),
            pltpu.VMEM((2,) + qkvw_h.shape, BF16),
            pltpu.VMEM((width, seq), BF16),
        )

    pl.run_scoped(
        back,
        pltpu.VMEM((seq // LANES * seq * 16, LANES), F32),
        pltpu.VMEM((seq, 2 * inner), BF16),
        pltpu.VMEM((seq, 2 * inner), BF16),
        pltpu.VMEM((seq, 2 * inner), BF16),
    )
    done = store(wide, gtok_h)
    for number in range(polls[0], 1 + max(number for number in plan if number != "tail")):
        run_steps(number)
    run_steps("tail")
    done.wait()
    for piece in kit.pieces:
        piece.finish()
    for copy in crossed[-4:]:
        copy().wait_send()
    for number in range(len(halves)):
        half(number).wait_send()


def layer(plan, bits, operands):
    tokens, qkvw, qvb, tab, outw, upw, upb, downw = operands[:8]
    seq, width = tokens.shape
    inner = qkvw.shape[2]
    units = upw.shape[1]
    heads = 2 * tab.shape[0]
    shape = jax.ShapeDtypeStruct
    here = pl.BlockSpec(memory_space=pltpu.VMEM)
    away = pl.BlockSpec(memory_space=pl.ANY)
    scalar = pl.BlockSpec(memory_space=pltpu.SMEM)
    rows = (3 * width * inner + inner * width + 2 * width * units) // inner
    lands = rows - (rows >> 4) + (bits - 4) * (rows >> 4)
    pieces = len(ORDERS["down"]) + len(ORDERS["up"]) + 4
    slots = pieces * (6 + bits)
    return pl.pallas_call(
        functools.partial(layer_kernel, plan, bits),
        out_shape=(
            shape((rows, inner), BF16),
            shape((seq, width), F32),
            shape((seq, width), BF16),
            shape((16, width), F32),
            shape(qkvw.shape, BF16),
            shape(outw.shape, BF16),
            shape(upw.shape, BF16),
            shape(downw.shape, BF16),
            shape((heads, seq, seq), BF16),
        ),
        in_specs=[away] * 10 + [here] * 7 + [scalar],
        out_specs=(away, away, away, here) + (away,) * 5,
        scratch_shapes=[
            pltpu.VMEM((rows, inner), BF16),
            pltpu.VMEM((rows // 3, inner), BF16),
            pltpu.VMEM((rows, inner), BF16),
            pltpu.VMEM((lands, inner), BF16),
            pltpu.VMEM((seq, width), BF16),
            pltpu.VMEM((2,) + qvb.shape, F32),
            pltpu.VMEM((2,) + tab.shape, F32),
            pltpu.VMEM(upb.shape, F32),
            pltpu.VMEM(upb.shape, F32),
            pltpu.VMEM((2, 1, units), F32),
            pltpu.VMEM((2,) + outw.shape, BF16),
            pltpu.VMEM((seq, 2 * inner), BF16),
            pltpu.VMEM((seq, 2 * inner), BF16),
            pltpu.VMEM((seq, 2 * inner), BF16),
            pltpu.VMEM((2 * inner, seq), BF16),
            pltpu.VMEM((heads, 8, seq), F32),
            pltpu.VMEM((seq, seq), BF16),
            pltpu.VMEM((seq, width), F32),
            pltpu.VMEM((seq, width), BF16),
            pltpu.VMEM((seq, width), BF16),
            pltpu.VMEM((2, 8, units), F32),
            pltpu.VMEM((bits + 1, 16, width), F32),
            pltpu.VMEM((bits + 1, 16, width), F32),
            pltpu.SemaphoreType.DMA((24,)),
            pltpu.SemaphoreType.DMA((8,)),
            pltpu.SemaphoreType.DMA((slots,)),
            pltpu.SemaphoreType.DMA((slots,)),
            pltpu.SemaphoreType.DMA((pieces,)),
            pltpu.SemaphoreType.DMA((pieces,)),
            pltpu.SemaphoreType.DMA((pieces,)),
            pltpu.SemaphoreType.DMA((bits + 1,)),
            pltpu.SemaphoreType.DMA((bits + 1,)),
            pltpu.SemaphoreType.DMA((7,)),
            pltpu.SemaphoreType.DMA((7,)),
        ],
        compiler_params=pltpu.CompilerParams(
            collective_id=0, has_side_effects=True, vmem_limit_bytes=VMEM_LIMIT
        ),
    )(*operands)


def finish_kernel(
    flat_h,
    out_h,
    gtok_h,
    small,
    out_f,
    gtok_f,
    mix_f,
    gqv,
    gtab,
    gout_f,
    goutb,
    gain1,
    shift1,
    up_f,
    gupb,
    down_f,
    gdownb,
    gain2,
    shift2,
    flat,
    mix,
    gout,
    up,
    down,
    gtok,
    out,
    in_sem,
    out_sem,
):
    rows, inner = flat.shape
    units, width = down.shape
    split = width // inner
    third = rows // 3
    copies = []
    tiles = units // 256
    span = 256 * split
    sizes = (
        [span] * tiles + [width] * (units // inner) + [split * inner] + [width] * 3
    )
    loads = []
    at = 0
    for number, size in enumerate(sizes):
        here = pl.ds(at, size)
        loads.append(pltpu.make_async_copy(flat_h.at[here, :], flat.at[here, :], in_sem.at[number]))
        loads[-1].start()
        at += size

    for source, target in ((gtok_h, gtok), (out_h, out)):
        loads.append(pltpu.make_async_copy(source, target, in_sem.at[len(loads)]))
        loads[-1].start()

    def store(source, target):
        copies.append(pltpu.make_async_copy(source, target, out_sem.at[len(copies)]))
        copies[-1].start()

    def wide(start, size):
        return flat[start : start + size, :].astype(F32)

    for tile in range(tiles):
        loads[tile].wait()
        here = slice(tile * 256, tile * 256 + 256)
        for side in range(split):
            down[here, side * inner : (side + 1) * inner] = wide(tile * span + side * 256, 256)
        here = pl.ds(tile * 256, 256)
        store(down.at[here, :], down_f.at[here, :])
    for part in range(units // inner):
        loads[tiles + part].wait()
        cols = pl.ds(part * inner, inner)
        up[:, cols] = wide(third + part * width, width)
        store(up.at[:, cols], up_f.at[:, cols])
    at = 2 * third
    loads[-6].wait()
    for side in range(split):
        gout[:, side * inner : (side + 1) * inner] = wide(at + side * inner, inner)
    store(gout, gout_f)
    at += split * inner
    for kind in range(3):
        loads[kind - 5].wait()
        mix[kind] = wide(at + kind * width, width)
        store(mix.at[kind], mix_f.at[kind])
    loads[-2].wait()
    store(gtok, gtok_f)
    loads[-1].wait()
    store(out, out_f)
    for number, vector in enumerate((goutb, gain1, shift1, gdownb, gain2, shift2)):
        vector[...] = small[number : number + 1, :].reshape(width)
    gupb[...] = jnp.concatenate(
        [small[6 + side : 7 + side, :] for side in range(units // width)], axis=1
    ).reshape(units)
    for kind in range(2):
        gqv[kind : kind + 1, :] = small[8:9, kind * inner : (kind + 1) * inner]
    gtab[...] = small[10 : 10 + gtab.shape[0], : gtab.shape[1]]
    for copy in copies:
        copy.wait()


def finish(flat, small, out, grad_tokens, width, units, heads):
    shape = jax.ShapeDtypeStruct
    here = pl.BlockSpec(memory_space=pltpu.VMEM)
    away = pl.BlockSpec(memory_space=pl.ANY)
    inner = flat.shape[1]
    vector = shape((width,), F32)
    got = pl.pallas_call(
        finish_kernel,
        out_shape=(
            shape(out.shape, BF16),
            shape(grad_tokens.shape, F32),
            shape((3, width, inner), F32),
            shape((2, inner), F32),
            shape((heads, 2 * LANES), F32),
            shape((inner, width), F32),
            vector,
            vector,
            vector,
            shape((width, units), F32),
            shape((units,), F32),
            shape((units, width), F32),
            vector,
            vector,
            vector,
        ),
        in_specs=[away] * 3 + [here],
        out_specs=(away, away, away, here, here, away, here, here, here, away, here, away)
        + (here,) * 3,
        scratch_shapes=[
            pltpu.VMEM(flat.shape, BF16),
            pltpu.VMEM((3, width, inner), F32),
            pltpu.VMEM((inner, width), F32),
            pltpu.VMEM((width, units), F32),
            pltpu.VMEM((units, width), F32),
            pltpu.VMEM(grad_tokens.shape, F32),
            pltpu.VMEM(out.shape, BF16),
            pltpu.SemaphoreType.DMA((units // 256 + units // inner + 6,)),
            pltpu.SemaphoreType.DMA((units // 256 + units // inner + 6,)),
        ],
        compiler_params=pltpu.CompilerParams(vmem_limit_bytes=VMEM_LIMIT),
    )(flat, out, grad_tokens, small)
    got = list(got)
    got[2] = jnp.transpose(got[2], (1, 0, 2))
    got[4] = got[4].T
    return tuple(got)


def order_of_steps(bits):
    pieces = len(ORDERS["down"]) + len(ORDERS["up"]) + 4
    plan = dict(PAUSES)
    known = {step for steps in PAUSES.values() for step in steps} | set(TAIL)
    more = tuple((pieces, step) for step in range(1, bits + 2) if (pieces, step) not in known)
    plan["tail"] = TAIL + more
    return plan


def on_device(
    dp,
    tokens,
    qkv_weight,
    qv_bias,
    rel_table,
    out_weight,
    out_bias,
    norm1_gain,
    norm1_bias,
    up_weight,
    up_bias,
    down_weight,
    down_bias,
    norm2_gain,
    norm2_bias,
    rel_bucket,
    query_len,
    key_mask,
    upstream,
):
    width = tokens.shape[1]
    units = up_weight.shape[1]
    bits = int(math.log2(dp))
    flat, grad_tokens, out, small = layer(
        order_of_steps(bits),
        bits,
        (
            tokens,
            jnp.transpose(qkv_weight, (1, 0, 2)),
            qv_bias,
            rel_table.T,
            out_weight,
            up_weight,
            up_bias,
            down_weight,
            upstream,
            rel_bucket,
            out_bias,
            norm1_gain,
            norm1_bias,
            down_bias,
            norm2_gain,
            norm2_bias,
            key_mask,
            query_len,
        ),
    )[:4]
    return finish(flat, small, out, grad_tokens, width, units, rel_table.shape[1])


def solution(mesh):
    rows = P(("dp", "tensor"), None)
    whole = P()
    in_specs = (
        rows,
        P(None, None, "tensor"),
        P(None, "tensor"),
        P(None, "tensor"),
        P("tensor", None),
        whole,
        whole,
        whole,
        P(None, "tensor"),
        P("tensor"),
        P("tensor", None),
        whole,
        whole,
        whole,
        whole,
        P("dp"),
        P("dp", None),
        rows,
    )
    out_specs = (
        rows,
        rows,
        P(None, None, "tensor"),
        P(None, "tensor"),
        P(None, "tensor"),
        P("tensor", None),
        whole,
        whole,
        whole,
        P(None, "tensor"),
        P("tensor"),
        P("tensor", None),
        whole,
        whole,
        whole,
    )
    return jax.shard_map(
        functools.partial(on_device, mesh.shape["dp"]),
        mesh=mesh,
        in_specs=in_specs,
        out_specs=out_specs,
        check_vma=False,
    )
```

time: 193 us -> 177 us (0.917)
  Pallas kernels: 192 us -> 176 us
    pallas_call x2 -> x1, Pallas kernels: 182 us -> 166 us  [layer(): pl.pallas_call(functools.partial(layer_kernel, plan, bits), out_shape=(sh...]
where the time goes in v3:
time: 177 us
  Pallas kernels  176 us (99%)
    pallas_call x1, Pallas kernels, layer(): pl.pallas_call(functools.partial(layer_kernel, plan, bits), out_shape=(sh...  166 us
    pallas_call x1, Pallas kernels, finish(): pl.pallas_call(finish_kernel, out_shape=(shape(out.shape, BF16), shape(gr...  10.4 us

profile of v3, /device:TPU:0, one launch (start us, length us, event | category | flops | bytes accessed | tf_op | source)
XLA Modules:
  0.0 176.8 jit_solution(6084905741470668594)
XLA Ops:
  0.7 165.6 %shard_map.289 = (bf16[9216,384]{1,0:T(8,128)(2,1)}, f32[512,768]{1,0:T(8,128)}, bf16[512,768]{1,0:T(8,128)(2,1)}, f32[16,768]{1,0:T(8,128)}, bf16[3,768,384]{2,...) custom-call(bf16[512,768]{1,0:T(8,128)(2,1)} %tokens_h.1, ...), custom_call_target="tpu_custom_call" | custom-call | tf_op jit(solution)/shard_map/pallas_call | solution.py:1054
  166.2 10.4 %shard_map.290 = (bf16[512,768]{1,0:T(8,128)(2,1)}, f32[512,768]{1,0:T(8,128)}, f32[3,768,384]{2,1,0:T(8,128)}, f32[2,384]{1,0:T(2,128)}, f32[6,256]{1,0:T(8,128...) custom-call(bf16[9216,384]{1,0:T(8,128)(2,1)} %get-tuple-element.34., ...), custom_call_target="tpu_custom_call" | custom-call | tf_op jit(solution)/shard_map/pallas_call | solution.py:1214
